TPU v7x, 256 devices: a whole 4x4x8 slice. The times are simulated.
256 devices in a mesh: rep: 32 (over z, x), sub: 8 (over y, core).
Axes of the slice: x: 4, y: 4, z: 8, core: 2. Of those that a mesh axis runs over, the one named last changes fastest.
Arguments:
- pre_act: bfloat16 [150528, 4096], P(('rep', 'sub')), may hold values from -6 to 6
- upstream: bfloat16 [150528, 1024], P(('rep', 'sub')), may hold values from -0.24707031 to 0.24707031
- layer_scale: float32 [1024], replicated, may hold values from 0.25 to 4
- initial_q: float32 [8, 1024], replicated, may hold values from -6 to 6
Outputs:
- basis_out: float32 [8, 4096], replicated
- q_out: float32 [8, 1024], replicated
- residual: bfloat16 [1048576, 1024], P(('rep', 'sub'))
All inputs are finite; a program needn't handle non-finite values.
Results may differ from a plain program's by a relative error of at most 0.0061.
Values sent between devices are 32-bit elements; how exact they have to be, the bound alone decides.
No kernel may reach another device: no remote copies, remote signals or barrier semaphores. Data moves between devices by JAX's collectives and lax.ppermute only.
A program may use at most 128 MiB of HBM per device.

v0:
```python
import math

import jax
import jax.numpy as jnp
from jax import lax
from jax.sharding import PartitionSpec as P


def body(pre_act, upstream, layer_scale, initial_q):
    highest = lax.Precision.HIGHEST
    devices = lax.axis_size(("rep", "sub"))
    hidden_units = pre_act.shape[1]
    activated = jax.nn.gelu(pre_act.astype(jnp.float32), approximate=False).astype(jnp.bfloat16)
    scaled = (upstream.astype(jnp.float32) * layer_scale[None, :]).astype(jnp.bfloat16)
    gradient = lax.dot_general(
        activated, scaled, (((0,), (0,)), ((), ())), preferred_element_type=jnp.float32
    )
    p_local = lax.dot_general(
        initial_q,
        gradient,
        (((1,), (1,)), ((), ())),
        precision=highest,
        preferred_element_type=jnp.float32,
    )
    p_total = lax.psum(p_local, ("rep", "sub"))
    gram_matrix = jnp.dot(p_total, p_total.T, precision=highest)
    chol_lower = jnp.linalg.cholesky(gram_matrix)
    ortho_basis = jax.scipy.linalg.solve_triangular(chol_lower, p_total, lower=True)
    q_local = jnp.dot(ortho_basis, gradient, precision=highest)
    q_total = lax.psum(q_local, ("rep", "sub"))
    approx = lax.dot_general(
        ortho_basis,
        q_local,
        (((0,), (0,)), ((), ())),
        precision=highest,
        preferred_element_type=jnp.float32,
    )
    residual = (gradient - approx).astype(jnp.bfloat16)
    basis_out = ortho_basis * jnp.float32(math.sqrt(hidden_units))
    q_out = q_total / jnp.float32(math.sqrt(devices))
    return (basis_out, q_out, residual)


def solution(mesh):
    in_specs = (P(("rep", "sub"), None), P(("rep", "sub"), None), P(), P())
    out_specs = (P(), P(), P(("rep", "sub"), None))
    return jax.shard_map(body, mesh=mesh, in_specs=in_specs, out_specs=out_specs, check_vma=False)
```

profile of v0, /device:TPU:1, one launch (start us, length us, event | category | flops | bytes accessed | tf_op | source)
XLA Modules:
  0.0 419.7 jit_solution(10645105729006746569)
XLA Ops:
  7.2 0.0 copy-start
  7.2 0.0 all-reduce.2.cloned.1.call-start
  7.2 28.6 %fusion.31 = f32[4096,1024]{1,0:T(8,128)S(1)} fusion(bf16[588,4096]{1,0:T(8,128)(2,1)} %param.4, bf16[588,1024]{1,0:T(8,128)(2,1)} %param.5, f32[1024]{0:T(1024)} %param.6), kind=kOutput, calls=%fused_computation.35 | convolution fusion | flops 5093265408 | bytes 22802432 | tf_op jit(solution)/shard_map/dot_general | solution.py:15
  35.9 0.0 copy-start.1
  35.9 5.7 %copy-done.1 = f32[4096,1024]{1,0:T(8,128)} copy-done((f32[4096,1024]{1,0:T(8,128)}, f32[4096,1024]{1,0:T(8,128)S(1)}, u32[]{:S(2)}) %copy-start.1) | copy-done | bytes 16777240
  41.6 0.0 copy-done
  41.6 14.9 %convolution_bitcast_fusion = f32[8,4096]{1,0:T(8,128)} fusion(f32[4096,1024]{1,0:T(8,128)S(1)} %fusion.31, f32[8,1024]{1,0:T(8,128)S(1)} %copy-done), kind=kOutput, calls=%fused_computation.66 | convolution fusion | flops 402653184 | bytes 16941056 | tf_op jit(solution)/shard_map/dot_general | solution.py:18
  56.5 0.0 all-reduce.2.cloned.1.call-update
  56.5 244.9 %all-reduce.2.cloned.1.call-done = f32[8,4096]{1,0:T(8,128)} async-done(((f32[8,4096]{1,0:T(8,128)}), f32[8,4096]{1,0:T(8,128)}) %all-reduce.2.cloned.1.call-update) | async-done | bytes 131088 | tf_op jit(solution)/shard_map/psum | solution.py:25
  301.4 1.3 fusion.98
  302.7 0.1 copy.7
  302.8 0.7 cholesky.16
  303.5 0.1 select_reduce_fusion
  303.6 0.6 compare_reduce_fusion
  304.3 0.9 fusion.64
  305.1 0.6 custom-call.7
  305.8 0.0 copy-start.2
  305.8 2.0 broadcast_multiply_fusion
  307.8 12.1 %fusion.99 = f32[8,1024]{1,0:T(8,128)S(1)} fusion(f32[8,4096]{1,0:T(8,128)S(1)} %get-tuple-element.4, f32[4096,1024]{1,0:T(8,128)} %copy-done.1), kind=kOutput, calls=%fused_computation.112 | convolution fusion | flops 402653184 | bytes 16941056 | tf_op jit(solution)/shard_map/dot_general | solution.py:29
  319.9 0.0 copy-done.2
  319.9 16.3 %subtract_convert_fusion = bf16[4096,1024]{1,0:T(8,128)(2,1)} fusion(f32[4096,1024]{1,0:T(8,128)S(1)} %copy-done.2, f32[8,4096]{1,0:T(8,128)S(1)} %get-tuple-element.4, f32[8,1024]{1,0:T(8,128)S(1)} %fusion.99), kind=kOutput, calls=%fused_computation | convolution fusion | flops 411041792 | bytes 25329664 | tf_op jit(solution)/shard_map/dot_general | solution.py:31
  336.2 76.0 %psum.15 = f32[8,1024]{1,0:T(8,128)S(1)} all-reduce(f32[8,1024]{1,0:T(8,128)S(1)} %fusion.99), channel_id=1, replica_groups=mesh['rep'=32,'sub'=8] {'rep','sub'}, use_global_device_ids=true, to_apply=%region_3.4 | all-reduce | flops 8192 | bytes 65536 | tf_op jit(solution)/shard_map/psum | solution.py:30
  412.2 0.6 broadcast_multiply_fusion.1
  (1 shorter events, 0.0 us)
Async XLA Ops:
  7.2 34.4 %copy-start = (f32[8,1024]{1,0:T(8,128)S(1)}, f32[8,1024]{1,0:T(8,128)}, u32[]{:S(2)}) copy-start(f32[8,1024]{1,0:T(8,128)} %param.7) | copy-start | bytes 98308
  7.2 294.2 %all-reduce.2.cloned.1.call-start = ((), (), s32[]{:S(2)}) async-start(), calls=%async_computation | async-start | bytes 262144 | tf_op jit(solution)/shard_map/psum | solution.py:25
  35.9 5.7 %copy-start.1 = (f32[4096,1024]{1,0:T(8,128)}, f32[4096,1024]{1,0:T(8,128)S(1)}, u32[]{:S(2)}) copy-start(f32[4096,1024]{1,0:T(8,128)S(1)} %fusion.31) | copy-start | bytes 50331652
  305.8 14.2 %copy-start.2 = (f32[4096,1024]{1,0:T(8,128)S(1)}, f32[4096,1024]{1,0:T(8,128)}, u32[]{:S(2)}) copy-start(f32[4096,1024]{1,0:T(8,128)} %copy-done.1) | copy-start | bytes 50331652
Sparse Core Ops, SparseCore 0:
  56.7 244.6 all-reduce.1
where the time goes:
time: 420 us
  waiting for transfers between devices  245 us (58%)
  blocking collectives  76 us (18%)
  matrix products  75.3 us (18%)
  between operations  14.1 us (3%)
  local copies, waits for them, and re-layouts  5.79 us (1%)
    psum x1, waiting for transfers between devices, body(): p_total = lax.psum(p_local, ('rep', 'sub'))  245 us
    psum x1, blocking collectives, body(): q_total = lax.psum(q_local, ('rep', 'sub'))  76 us
    dot_general x1, matrix products, body(): lax.dot_general(activated, scaled, (((0,), (0,)), ((), ())), preferred_el...  28.6 us
    dot_general x1, matrix products, body(): lax.dot_general(ortho_basis, q_local, (((0,), (0,)), ((), ())), precision...  16.3 us
    dot_general x1, matrix products, body(): lax.dot_general(initial_q, gradient, (((1,), (1,)), ((), ())), precision=...  14.9 us
    dot_general x1, matrix products, body(): q_local = jnp.dot(ortho_basis, gradient, precision=highest)  12.1 us
  transfers between devices with their start and end apart: 1, of which 1 were waited for; matrix products, arithmetic and copies ran while one was open for 0% of the time, Pallas kernels for 0%

commit v1 on v0

v1 whole, which is shorter than its diff:
```python
import functools
import math

import jax
import jax.numpy as jnp
from jax import lax
from jax.experimental import pallas as pl
from jax.experimental.pallas import tpu as pltpu
from jax.sharding import Mesh
from jax.sharding import PartitionSpec as P

f32, bf16 = jnp.float32, jnp.bfloat16
ROWS, HID, WID, RANK, LANES = 588, 4096, 1024, 8, 128
PLANE = ("x", "y", "c")


def split3(v):
    a = v.astype(bf16)
    r = v - a.astype(f32)
    b = r.astype(bf16)
    c = (r - b.astype(f32)).astype(bf16)
    return jnp.concatenate([a, b, c], axis=0)


def fold3(v):
    return v[0:RANK] + v[RANK : 2 * RANK] + v[2 * RANK : 3 * RANK]


def gelu(v):
    return 0.5 * v * (1.0 + lax.erf(v * math.sqrt(0.5)))


def front_kernel(cols, slab, pre, up, scale, q, act, scaled, p_out, reduced):
    @pl.when(pl.program_id(0) == 0)
    def _():
        scaled[...] = (up[...].astype(f32) * scale[...]).astype(bf16)
        r = lax.dot_general(
            split3(q[...]), scaled[...], (((1,), (1,)), ((), ())), preferred_element_type=f32
        )
        reduced[...] = split3(fold3(r))

    full = ROWS // slab

    def step(i, carry):
        rows = pl.ds(pl.multiple_of(i * slab, slab), slab)
        act[rows, :] = gelu(pre[rows, :].astype(f32)).astype(bf16)
        return carry

    lax.fori_loop(0, full, step, 0)
    act[full * slab : ROWS, :] = gelu(pre[full * slab : ROWS, :].astype(f32)).astype(bf16)
    part = fold3(jnp.dot(reduced[...], act[...], preferred_element_type=f32))
    for j in range(cols // LANES):
        p_out[j] = part[:, j * LANES : (j + 1) * LANES]


def front(pre, up, scale, q, cols=1024, slab=16):
    return pl.pallas_call(
        functools.partial(front_kernel, cols, slab),
        grid=(HID // cols,),
        in_specs=[
            pl.BlockSpec((ROWS, cols), lambda i: (0, i)),
            pl.BlockSpec((ROWS, WID), lambda i: (0, 0)),
            pl.BlockSpec((1, WID), lambda i: (0, 0)),
            pl.BlockSpec((RANK, WID), lambda i: (0, 0)),
        ],
        out_specs=[
            pl.BlockSpec((ROWS, cols), lambda i: (0, i)),
            pl.BlockSpec((ROWS, WID), lambda i: (0, 0)),
            pl.BlockSpec((cols // LANES, RANK, LANES), lambda i: (i, 0, 0)),
        ],
        out_shape=[
            jax.ShapeDtypeStruct((ROWS, HID), bf16),
            jax.ShapeDtypeStruct((ROWS, WID), bf16),
            jax.ShapeDtypeStruct((HID // LANES, RANK, LANES), f32),
        ],
        scratch_shapes=[pltpu.VMEM((3 * RANK, ROWS), bf16)],
        compiler_params=pltpu.CompilerParams(vmem_limit_bytes=24 << 20),
        cost_estimate=pl.CostEstimate(flops=60 * ROWS * HID, bytes_accessed=10 << 20, transcendentals=ROWS * HID),
        name="front",
    )(pre, up, scale, q)


def project_kernel(act, scaled, p, u_out):
    flat = jnp.concatenate([p[j] for j in range(HID // LANES)], axis=1)
    c = lax.dot_general(
        split3(flat), act[...], (((1,), (1,)), ((), ())), preferred_element_type=f32
    )
    u = fold3(jnp.dot(split3(fold3(c)), scaled[...], preferred_element_type=f32))
    for j in range(WID // LANES):
        u_out[j] = u[:, j * LANES : (j + 1) * LANES]


def project(act, scaled, p):
    return pl.pallas_call(
        project_kernel,
        out_shape=jax.ShapeDtypeStruct((WID // LANES, RANK, LANES), f32),
        compiler_params=pltpu.CompilerParams(vmem_limit_bytes=24 << 20),
        cost_estimate=pl.CostEstimate(flops=48 * ROWS * HID, bytes_accessed=6 << 20, transcendentals=0),
        name="project",
    )(act, scaled, p)


def ortho_kernel(p, u, basis, inverse, lhs, rhs):
    flat = jnp.concatenate([p[j] for j in range(HID // LANES)], axis=1)
    parts = split3(flat)
    g = lax.dot_general(parts, parts, (((1,), (1,)), ((), ())), preferred_element_type=f32)
    g = fold3(g)
    gram = g[:, 0:RANK] + g[:, RANK : 2 * RANK] + g[:, 2 * RANK : 3 * RANK]
    row = lax.broadcasted_iota(jnp.int32, (RANK, RANK), 0)
    col = lax.broadcasted_iota(jnp.int32, (RANK, RANK), 1)
    inv = jnp.where(row == col, 1.0, 0.0).astype(f32)
    for j in range(RANK):
        root = lax.rsqrt(gram[j : j + 1, j : j + 1])
        gram_row, inv_row = gram[j : j + 1, :] * root, inv[j : j + 1, :] * root
        factor = jnp.where(row[:, 0:1] > j, gram[:, j : j + 1] * root, 0.0)
        gram = jnp.where(row == j, gram_row, gram - factor * gram_row)
        inv = jnp.where(row == j, inv_row, inv - factor * inv_row)
    o = jnp.dot(inv, flat, precision=lax.Precision.HIGHEST, preferred_element_type=f32)
    u_flat = jnp.concatenate([u[j] for j in range(WID // LANES)], axis=1)
    q = jnp.dot(inv, u_flat, precision=lax.Precision.HIGHEST, preferred_element_type=f32)
    basis[...] = o * math.sqrt(HID)
    inverse[...] = inv
    o_hi = o.astype(bf16)
    o_lo = (o - o_hi.astype(f32)).astype(bf16)
    q_hi = q.astype(bf16)
    q_lo = (q - q_hi.astype(f32)).astype(bf16)
    lhs[...] = jnp.concatenate([o_hi, o_hi, o_lo], axis=0)
    rhs[...] = jnp.concatenate([q_hi, q_lo, q_hi], axis=0)


def ortho(p, u):
    return pl.pallas_call(
        ortho_kernel,
        out_shape=[
            jax.ShapeDtypeStruct((RANK, HID), f32),
            jax.ShapeDtypeStruct((RANK, RANK), f32),
            jax.ShapeDtypeStruct((3 * RANK, HID), bf16),
            jax.ShapeDtypeStruct((3 * RANK, WID), bf16),
        ],
        compiler_params=pltpu.CompilerParams(vmem_limit_bytes=8 << 20),
        cost_estimate=pl.CostEstimate(flops=1 << 24, bytes_accessed=1 << 20, transcendentals=0),
        name="ortho",
    )(p, u)


def residual_kernel(act, scaled, lhs, rhs, out):
    contract = (((0,), (0,)), ((), ()))
    acc = lax.dot_general(act[...], scaled[...], contract, preferred_element_type=f32)
    low = lax.dot_general(lhs[...], rhs[...], contract, preferred_element_type=f32)
    out[...] = (acc - low).astype(bf16)


def residual_of(act, scaled, lhs, rhs, rows=512):
    return pl.pallas_call(
        residual_kernel,
        grid=(HID // rows,),
        in_specs=[
            pl.BlockSpec((ROWS, rows), lambda i: (0, i)),
            pl.BlockSpec((ROWS, WID), lambda i: (0, 0)),
            pl.BlockSpec((3 * RANK, rows), lambda i: (0, i)),
            pl.BlockSpec((3 * RANK, WID), lambda i: (0, 0)),
        ],
        out_specs=pl.BlockSpec((rows, WID), lambda i: (i, 0)),
        out_shape=jax.ShapeDtypeStruct((HID, WID), bf16),
        compiler_params=pltpu.CompilerParams(vmem_limit_bytes=24 << 20),
        cost_estimate=pl.CostEstimate(flops=2 * ROWS * HID * WID, bytes_accessed=14 << 20, transcendentals=0),
        name="residual",
    )(act, scaled, lhs, rhs)


def finish_kernel(inverse, u, q_out, *, devices):
    flat = jnp.concatenate([u[j] for j in range(WID // LANES)], axis=1)
    q = jnp.dot(inverse[...], flat, precision=lax.Precision.HIGHEST, preferred_element_type=f32)
    q_out[...] = q * (1.0 / math.sqrt(devices))


def finish(inverse, u, devices):
    return pl.pallas_call(
        functools.partial(finish_kernel, devices=devices),
        out_shape=jax.ShapeDtypeStruct((RANK, WID), f32),
        compiler_params=pltpu.CompilerParams(vmem_limit_bytes=4 << 20),
        name="finish",
    )(inverse, u)


def exchange(v, axis, partner):
    n = lax.axis_size(axis)
    return v + lax.ppermute(v, axis, [(i, partner(i, n)) for i in range(n)])


def even_pair(i, n):
    return i ^ 1


def odd_pair(i, n):
    return (i + 1) % n if i % 2 else (i - 1) % n


def far_pair(i, n):
    return {1: 6, 6: 1, 2: 5, 5: 2, 3: 0, 0: 3, 4: 7, 7: 4}[i]


def reduce_all_to_all(v, axes, n):
    got = lax.all_to_all(v, axes, 0, 0, tiled=True)
    return jnp.sum(got.reshape((n, v.shape[0] // n) + v.shape[1:]), axis=0)


def gather_all_to_all(v, axes, n):
    copies = jnp.broadcast_to(v[None], (n,) + v.shape).reshape((n * v.shape[0],) + v.shape[1:])
    return lax.all_to_all(copies, axes, 0, 0, tiled=True)


def body(pre_act, upstream, layer_scale, initial_q):
    act, scaled, p_local = front(pre_act, upstream, layer_scale.reshape(1, WID), initial_q)
    with jax.named_scope("sum_p"):
        part = reduce_all_to_all(p_local, PLANE, 32)
        part = jnp.sum(gather_all_to_all(part, "z", 8), axis=0, keepdims=True)
        p_total = gather_all_to_all(part, PLANE, 32)
    u = project(act, scaled, p_total)
    basis_out, inverse, lhs, rhs = ortho(p_total, u)
    residual = residual_of(act, scaled, lhs, rhs)
    with jax.named_scope("sum_u"):
        t = exchange(u, "c", even_pair)
        for axis in ("y", "x", "z"):
            t = exchange(t, axis, even_pair)
            t = exchange(t, axis, odd_pair)
        t = exchange(t, "z", far_pair)
    q_out = finish(inverse, t, 256)
    return (basis_out, q_out, residual)


def solution(mesh):
    fine = Mesh(mesh.devices.reshape(8, 4, 4, 2), ("z", "x", "y", "c"))
    split = P(("z", "x", "y", "c"), None)
    return jax.shard_map(
        body, mesh=fine, in_specs=(split, split, P(), P()), out_specs=(P(), P(), split), check_vma=False
    )
```

time: 420 us -> 101 us (0.24)
  the two profiles are of different devices: /device:TPU:1 before, /device:TPU:96 now
where the time goes in v1:
time: 101 us
  blocking collectives  38.4 us (38%)
  Pallas kernels  22.2 us (22%)
  waiting for transfers between devices  20.8 us (21%)
  local copies, waits for them, and re-layouts  9.71 us (10%)
  starting transfers between devices  9.04 us (9%)
    all_to_all x2, blocking collectives, gather_all_to_all(): return lax.all_to_all(copies, axes, 0, 0, tiled=True)  23.5 us
    ppermute x8, waiting for transfers between devices, exchange(): return v + lax.ppermute(v, axis, [(i, partner(i, n)) for i in range(n)])  20.8 us
    all_to_all x1, blocking collectives, reduce_all_to_all(): got = lax.all_to_all(v, axes, 0, 0, tiled=True)  15 us
    pallas_call x1, Pallas kernels, residual_of(): pl.pallas_call(residual_kernel, grid=(HID // rows,), in_specs=[pl.BlockSp...  11.7 us
    unnamed x12, local copies, waits for them, and re-layouts  9.69 us
    ppermute x8, starting transfers between devices, exchange(): return v + lax.ppermute(v, axis, [(i, partner(i, n)) for i in range(n)])  9.04 us
    pallas_call x1, Pallas kernels, front(): pl.pallas_call(functools.partial(front_kernel, cols, slab), grid=(HID //...  5.68 us
    pallas_call x1, Pallas kernels, ortho(): pl.pallas_call(ortho_kernel, out_shape=[jax.ShapeDtypeStruct((RANK, HID),...  2.12 us
  transfers between devices with their start and end apart: 8, of which 7 were waited for; matrix products, arithmetic and copies ran while one was open for 0% of the time, Pallas kernels for 14%

profile of v1, /device:TPU:96, one launch (start us, length us, event | category | flops | bytes accessed | tf_op | source)
XLA Modules:
  0.0 101.0 jit_solution(6317537457916891469)
XLA Ops:
  0.6 0.0 copy-start.2
  0.6 2.4 %copy-done.2 = bf16[588,4096]{1,0:T(8,128)(2,1)S(1)} copy-done((bf16[588,4096]{1,0:T(8,128)(2,1)S(1)}, bf16[588,4096]{1,0:T(8,128)(2,1)}, u32[]{:S(2)}) %copy-start.2) | copy-done | bytes 4816920
  3.0 0.0 copy-start.3
  3.0 1.3 %copy-done.3 = bf16[588,1024]{1,0:T(8,128)(2,1)S(1)} copy-done((bf16[588,1024]{1,0:T(8,128)(2,1)S(1)}, bf16[588,1024]{1,0:T(8,128)(2,1)}, u32[]{:S(2)}) %copy-start.3) | copy-done | bytes 1204248
  4.3 0.0 copy-start.4
  4.3 0.8 copy-done.4
  5.0 0.0 copy-start.5
  5.0 0.7 copy-done.5
  5.7 5.7 %front.1 = (bf16[588,4096]{1,0:T(8,128)(2,1)S(1)}, bf16[588,1024]{1,0:T(8,128)(2,1)S(1)}, f32[32,8,128]{2,1,0:T(8,128)S(1)}) custom-call(bf16[588,4096]{1,0:T(8,128)(2,1)S(1)} %copy-done.2, bf16[588,1024]{1,0:T(8,128)(2,1)S(1)} %copy-done.3, f32[1,1024]{1,0:T(1,128)S(1)} %bitcast.1, f32[8,1024]{1,0:T(8,128)S(1)} %copy-done.4), custom_call_target="tpu_custom_call" | custom-call | flops 144506880 | bytes 10485760 | tf_op jit(solution)/shard_map/front/pallas_call | solution.py:57
  11.4 0.0 copy-start
  11.4 2.2 %copy-done = bf16[588,4096]{1,0:T(8,128)(2,1)} copy-done((bf16[588,4096]{1,0:T(8,128)(2,1)}, bf16[588,4096]{1,0:T(8,128)(2,1)S(1)}, u32[]{:S(2)}) %copy-start) | copy-done | bytes 4816920
  13.7 15.0 %all_to_all.15 = f32[32,8,128]{2,1,0:T(8,128)S(1)} all-to-all(f32[32,8,128]{2,1,0:T(8,128)S(1)} %get-tuple-element.10), channel_id=1, replica_groups=mesh['z'=8,'x'=4,'y'=4,'c'=2] {'x','y','c'}, dimensions={0} | all-to-all | bytes 262144 | tf_op jit(solution)/shard_map/sum_p/all_to_all | solution.py:204
  28.7 12.2 %all_to_all.16 = f32[8,8,128]{2,1,0:T(8,128)S(1)} all-to-all(f32[8,8,128]{2,1,0:T(8,128)S(1)} %reshape.25), channel_id=1, replica_groups=mesh['z'=8,'x'=4,'y'=4,'c'=2] {'z'}, dimensions={0} | all-to-all | bytes 65536 | tf_op jit(solution)/shard_map/sum_p/all_to_all | solution.py:210
  40.9 11.3 %all_to_all.17.p = f32[32,8,128]{2,1,0:T(8,128)S(1)} all-to-all(f32[32,8,128]{2,1,0:T(8,128)S(1)} %reshape.26), channel_id=1, replica_groups=mesh['z'=8,'x'=4,'y'=4,'c'=2] {'x','y','c'}, dimensions={0} | all-to-all | bytes 262144 | tf_op jit(solution)/shard_map/sum_p/all_to_all | solution.py:210
  52.2 0.0 copy-start.1
  52.2 2.4 %copy-done.1 = bf16[588,4096]{1,0:T(8,128)(2,1)S(1)} copy-done((bf16[588,4096]{1,0:T(8,128)(2,1)S(1)}, bf16[588,4096]{1,0:T(8,128)(2,1)}, u32[]{:S(2)}) %copy-start.1) | copy-done | bytes 4816920
  54.5 1.9 %project.1.u = f32[8,8,128]{2,1,0:T(8,128)S(1)} custom-call(bf16[588,4096]{1,0:T(8,128)(2,1)S(1)} %copy-done.1, bf16[588,1024]{1,0:T(8,128)(2,1)S(1)} %get-tuple-element.12.scaled, f32[32,8,128]{2,1,0:T(8,128)S(1)} %all_to_all.17.p), custom_call_target="tpu_custom_call" | custom-call | flops 115605504 | bytes 6291456 | tf_op jit(solution)/shard_map/project/pallas_call | solution.py:94
  56.5 0.2 collective-permute-start
  56.7 1.1 %collective-permute-done = f32[8,8,128]{2,1,0:T(8,128)S(1)} collective-permute-done((f32[8,8,128]{2,1,0:T(8,128)S(1)}, f32[8,8,128]{2,1,0:T(8,128)S(1)}, u32[]{:S(2)}, u32[]{:S(2)}) %collective-permute-start) | collective-permute-done | bytes 32800 | tf_op jit(solution)/shard_map/sum_u/ppermute | solution.py:188
  57.8 0.5 collective-permute-start.1
  58.3 3.4 %collective-permute-done.1 = f32[8,8,128]{2,1,0:T(8,128)S(1)} collective-permute-done((f32[8,8,128]{2,1,0:T(8,128)S(1)}, f32[8,8,128]{2,1,0:T(8,128)S(1)}, u32[]{:S(2)}, u32[]{:S(2)}) %collective-permute-start.1) | collective-permute-done | bytes 32800 | tf_op jit(solution)/shard_map/sum_u/ppermute | solution.py:188
  61.7 1.2 %collective-permute-start.2 = (f32[8,8,128]{2,1,0:T(8,128)S(1)}, f32[8,8,128]{2,1,0:T(8,128)S(1)}, u32[]{:S(2)}, u32[]{:S(2)}) collective-permute-start(f32[8,8,128]{2,1,0:T(8,128)S(1)} %add.25), channel_id=1, source_target_pairs={{0,6},{2,4},{4,2},{6,0},{1,7},{3,5},{5,3},{7,1},{8,14},{10,12},{12... | collective-permute-start | bytes 98312 | tf_op jit(solution)/shard_map/sum_u/ppermute | solution.py:188
  62.9 3.9 %collective-permute-done.2 = f32[8,8,128]{2,1,0:T(8,128)S(1)} collective-permute-done((f32[8,8,128]{2,1,0:T(8,128)S(1)}, f32[8,8,128]{2,1,0:T(8,128)S(1)}, u32[]{:S(2)}, u32[]{:S(2)}) %collective-permute-start.2) | collective-permute-done | bytes 32800 | tf_op jit(solution)/shard_map/sum_u/ppermute | solution.py:188
  66.9 0.6 collective-permute-start.3
  67.4 3.3 %collective-permute-done.3 = f32[8,8,128]{2,1,0:T(8,128)S(1)} collective-permute-done((f32[8,8,128]{2,1,0:T(8,128)S(1)}, f32[8,8,128]{2,1,0:T(8,128)S(1)}, u32[]{:S(2)}, u32[]{:S(2)}) %collective-permute-start.3) | collective-permute-done | bytes 32800 | tf_op jit(solution)/shard_map/sum_u/ppermute | solution.py:188
  70.8 1.1 %collective-permute-start.4 = (f32[8,8,128]{2,1,0:T(8,128)S(1)}, f32[8,8,128]{2,1,0:T(8,128)S(1)}, u32[]{:S(2)}, u32[]{:S(2)}) collective-permute-start(f32[8,8,128]{2,1,0:T(8,128)S(1)} %add.27), channel_id=1, source_target_pairs={{0,24},{8,16},{16,8},{24,0},{1,25},{9,17},{17,9},{25,1},{2,26},{10... | collective-permute-start | bytes 98312 | tf_op jit(solution)/shard_map/sum_u/ppermute | solution.py:188
  71.9 4.0 %collective-permute-done.4 = f32[8,8,128]{2,1,0:T(8,128)S(1)} collective-permute-done((f32[8,8,128]{2,1,0:T(8,128)S(1)}, f32[8,8,128]{2,1,0:T(8,128)S(1)}, u32[]{:S(2)}, u32[]{:S(2)}) %collective-permute-start.4) | collective-permute-done | bytes 32800 | tf_op jit(solution)/shard_map/sum_u/ppermute | solution.py:188
  75.9 1.3 %collective-permute-start.5 = (f32[8,8,128]{2,1,0:T(8,128)S(1)}, f32[8,8,128]{2,1,0:T(8,128)S(1)}, u32[]{:S(2)}, u32[]{:S(2)}) collective-permute-start(f32[8,8,128]{2,1,0:T(8,128)S(1)} %add.28), channel_id=1, source_target_pairs={{0,32},{32,0},{64,96},{96,64},{128,160},{160,128},{192,224},{224,1... | collective-permute-start | bytes 98312 | tf_op jit(solution)/shard_map/sum_u/ppermute | solution.py:188
  77.3 2.6 %collective-permute-done.5 = f32[8,8,128]{2,1,0:T(8,128)S(1)} collective-permute-done((f32[8,8,128]{2,1,0:T(8,128)S(1)}, f32[8,8,128]{2,1,0:T(8,128)S(1)}, u32[]{:S(2)}, u32[]{:S(2)}) %collective-permute-start.5) | collective-permute-done | bytes 32800 | tf_op jit(solution)/shard_map/sum_u/ppermute | solution.py:188
  79.8 0.5 collective-permute-start.6
  80.4 2.1 %ortho.1 = (f32[8,4096]{1,0:T(8,128)}, f32[8,8]{1,0:T(8,128)S(1)}, bf16[24,4096]{1,0:T(8,128)(2,1)S(1)}, bf16[24,1024]{1,0:T(8,128)(2,1)S(1)}) custom-call(f32[32,8,128]{2,1,0:T(8,128)S(1)} %all_to_all.17.p, f32[8,8,128]{2,1,0:T(8,128)S(1)} %project.1.u), custom_call_target="tpu_custom_call" | custom-call | flops 16777216 | bytes 1048576 | tf_op jit(solution)/shard_map/ortho/pallas_call | solution.py:132
  82.5 2.5 %collective-permute-done.6 = f32[8,8,128]{2,1,0:T(8,128)S(1)} collective-permute-done((f32[8,8,128]{2,1,0:T(8,128)S(1)}, f32[8,8,128]{2,1,0:T(8,128)S(1)}, u32[]{:S(2)}, u32[]{:S(2)}) %collective-permute-start.6) | collective-permute-done | bytes 32800 | tf_op jit(solution)/shard_map/sum_u/ppermute | solution.py:188
  85.0 3.5 %collective-permute-start.7 = (f32[8,8,128]{2,1,0:T(8,128)S(1)}, f32[8,8,128]{2,1,0:T(8,128)S(1)}, u32[]{:S(2)}, u32[]{:S(2)}) collective-permute-start(f32[8,8,128]{2,1,0:T(8,128)S(1)} %add.30), channel_id=1, source_target_pairs={{0,96},{32,192},{64,160},{96,0},{128,224},{160,64},{192,32},{224,1... | collective-permute-start | bytes 98312 | tf_op jit(solution)/shard_map/sum_u/ppermute | solution.py:188
  88.5 11.7 %residual.1 = bf16[4096,1024]{1,0:T(8,128)(2,1)} custom-call(bf16[588,4096]{1,0:T(8,128)(2,1)S(1)} %copy-done.1, bf16[588,1024]{1,0:T(8,128)(2,1)S(1)} %get-tuple-element.12.scaled, bf16[24,4096]{1,0:T(8,128)(2,1)S(1)} %get-tuple-element.15.lhs, bf16[24,1024]{1,0:T(8,128)(2,1)S(1)} %get-tuple-element.16.rhs), custom_call_target="tpu_custom_call" | custom-call | flops 4932501504 | bytes 14680064 | tf_op jit(solution)/shard_map/residual/pallas_call | solution.py:154
  100.2 0.0 collective-permute-done.7
  100.2 0.8 finish.1
  (12 shorter events, 0.1 us)
Async XLA Ops:
  0.6 2.4 %copy-start.2 = (bf16[588,4096]{1,0:T(8,128)(2,1)S(1)}, bf16[588,4096]{1,0:T(8,128)(2,1)}, u32[]{:S(2)}) copy-start(bf16[588,4096]{1,0:T(8,128)(2,1)} %pre.1) | copy-start | bytes 14450692
  3.0 1.3 %copy-start.3 = (bf16[588,1024]{1,0:T(8,128)(2,1)S(1)}, bf16[588,1024]{1,0:T(8,128)(2,1)}, u32[]{:S(2)}) copy-start(bf16[588,1024]{1,0:T(8,128)(2,1)} %up.1) | copy-start | bytes 3612676
  4.3 0.8 copy-start.4
  5.0 0.7 copy-start.5
  11.4 2.2 %copy-start = (bf16[588,4096]{1,0:T(8,128)(2,1)}, bf16[588,4096]{1,0:T(8,128)(2,1)S(1)}, u32[]{:S(2)}) copy-start(bf16[588,4096]{1,0:T(8,128)(2,1)S(1)} %get-tuple-element.11.act) | copy-start | bytes 14450692
  52.2 2.4 %copy-start.1 = (bf16[588,4096]{1,0:T(8,128)(2,1)S(1)}, bf16[588,4096]{1,0:T(8,128)(2,1)}, u32[]{:S(2)}) copy-start(bf16[588,4096]{1,0:T(8,128)(2,1)} %copy-done) | copy-start | bytes 14450692
  56.5 1.3 %collective-permute-start = (f32[8,8,128]{2,1,0:T(8,128)S(1)}, f32[8,8,128]{2,1,0:T(8,128)S(1)}, u32[]{:S(2)}, u32[]{:S(2)}) collective-permute-start(f32[8,8,128]{2,1,0:T(8,128)S(1)} %project.1.u), channel_id=1, source_target_pairs={{0,1},{1,0},{2,3},{3,2},{4,5},{5,4},{6,7},{7,6},{8,9},{9,8},{10,11... | collective-permute-start | bytes 98312 | tf_op jit(solution)/shard_map/sum_u/ppermute | solution.py:188
  57.8 3.9 %collective-permute-start.1 = (f32[8,8,128]{2,1,0:T(8,128)S(1)}, f32[8,8,128]{2,1,0:T(8,128)S(1)}, u32[]{:S(2)}, u32[]{:S(2)}) collective-permute-start(f32[8,8,128]{2,1,0:T(8,128)S(1)} %add.24), channel_id=1, source_target_pairs={{0,2},{2,0},{4,6},{6,4},{1,3},{3,1},{5,7},{7,5},{8,10},{10,8},{12,... | collective-permute-start | bytes 98312 | tf_op jit(solution)/shard_map/sum_u/ppermute | solution.py:188
  61.7 5.1 %collective-permute-start.2 = (f32[8,8,128]{2,1,0:T(8,128)S(1)}, f32[8,8,128]{2,1,0:T(8,128)S(1)}, u32[]{:S(2)}, u32[]{:S(2)}) collective-permute-start(f32[8,8,128]{2,1,0:T(8,128)S(1)} %add.25), channel_id=1, source_target_pairs={{0,6},{2,4},{4,2},{6,0},{1,7},{3,5},{5,3},{7,1},{8,14},{10,12},{12... | collective-permute-start | bytes 98312 | tf_op jit(solution)/shard_map/sum_u/ppermute | solution.py:188
  66.9 3.9 %collective-permute-start.3 = (f32[8,8,128]{2,1,0:T(8,128)S(1)}, f32[8,8,128]{2,1,0:T(8,128)S(1)}, u32[]{:S(2)}, u32[]{:S(2)}) collective-permute-start(f32[8,8,128]{2,1,0:T(8,128)S(1)} %add.26), channel_id=1, source_target_pairs={{0,8},{8,0},{16,24},{24,16},{1,9},{9,1},{17,25},{25,17},{2,10},{10... | collective-permute-start | bytes 98312 | tf_op jit(solution)/shard_map/sum_u/ppermute | solution.py:188
  70.8 5.1 %collective-permute-start.4 = (f32[8,8,128]{2,1,0:T(8,128)S(1)}, f32[8,8,128]{2,1,0:T(8,128)S(1)}, u32[]{:S(2)}, u32[]{:S(2)}) collective-permute-start(f32[8,8,128]{2,1,0:T(8,128)S(1)} %add.27), channel_id=1, source_target_pairs={{0,24},{8,16},{16,8},{24,0},{1,25},{9,17},{17,9},{25,1},{2,26},{10... | collective-permute-start | bytes 98312 | tf_op jit(solution)/shard_map/sum_u/ppermute | solution.py:188
  75.9 3.9 %collective-permute-start.5 = (f32[8,8,128]{2,1,0:T(8,128)S(1)}, f32[8,8,128]{2,1,0:T(8,128)S(1)}, u32[]{:S(2)}, u32[]{:S(2)}) collective-permute-start(f32[8,8,128]{2,1,0:T(8,128)S(1)} %add.28), channel_id=1, source_target_pairs={{0,32},{32,0},{64,96},{96,64},{128,160},{160,128},{192,224},{224,1... | collective-permute-start | bytes 98312 | tf_op jit(solution)/shard_map/sum_u/ppermute | solution.py:188
  79.8 5.1 %collective-permute-start.6 = (f32[8,8,128]{2,1,0:T(8,128)S(1)}, f32[8,8,128]{2,1,0:T(8,128)S(1)}, u32[]{:S(2)}, u32[]{:S(2)}) collective-permute-start(f32[8,8,128]{2,1,0:T(8,128)S(1)} %add.29), channel_id=1, source_target_pairs={{0,224},{32,64},{64,32},{96,128},{128,96},{160,192},{192,160},{224... | collective-permute-start | bytes 98312 | tf_op jit(solution)/shard_map/sum_u/ppermute | solution.py:188
  85.0 15.2 %collective-permute-start.7 = (f32[8,8,128]{2,1,0:T(8,128)S(1)}, f32[8,8,128]{2,1,0:T(8,128)S(1)}, u32[]{:S(2)}, u32[]{:S(2)}) collective-permute-start(f32[8,8,128]{2,1,0:T(8,128)S(1)} %add.30), channel_id=1, source_target_pairs={{0,96},{32,192},{64,160},{96,0},{128,224},{160,64},{192,32},{224,1... | collective-permute-start | bytes 98312 | tf_op jit(solution)/shard_map/sum_u/ppermute | solution.py:188

commit v2 on v1

v2 whole, which is shorter than its diff:
```python
import functools
import math

import jax
import jax.numpy as jnp
from jax import lax
from jax.experimental import pallas as pl
from jax.experimental.pallas import tpu as pltpu
from jax.sharding import Mesh
from jax.sharding import PartitionSpec as P

f32, bf16 = jnp.float32, jnp.bfloat16
ROWS, HID, WID, RANK, LANES = 588, 4096, 1024, 8, 128
EVEN, AUG = 592, 624
SPLIT = 3
FRONT_LIMIT = 52 << 20
RES_LIMIT = 50 << 20
PIECE_FLOPS = 2 * ROWS * HID * WID // 8
PLANE = ("x", "y", "c")


def split3(v):
    a = v.astype(bf16)
    r = v - a.astype(f32)
    b = r.astype(bf16)
    c = (r - b.astype(f32)).astype(bf16)
    return jnp.concatenate([a, b, c], axis=0)


def fold3(v):
    return v[0:RANK] + v[RANK : 2 * RANK] + v[2 * RANK : 3 * RANK]


def gelu(v):
    return 0.5 * v * (1.0 + lax.erf(v * math.sqrt(0.5)))


def front_kernel(chunks, cols, slab, pre_h, up_h, scale_h, q_h, act, act_h, scaled, p_out, pre, up, scale, q, reduced, sem, sem_s, sem_o):
    wide = HID // chunks

    def load(c):
        where = (slice(None), slice(c * wide, (c + 1) * wide))
        return pltpu.make_async_copy(pre_h.at[where], pre.at[where], sem.at[c])

    small = [
        pltpu.make_async_copy(q_h, q, sem_s.at[0]),
        pltpu.make_async_copy(scale_h, scale, sem_s.at[1]),
        pltpu.make_async_copy(up_h, up, sem_s.at[2]),
    ]
    load(0).start()
    for copy in small:
        copy.start()
    for c in range(1, chunks):
        load(c).start()
    act[EVEN - 16 : EVEN, :] = jnp.zeros((16, HID), bf16)
    scaled[EVEN - 16 : EVEN, :] = jnp.zeros((16, WID), bf16)

    def store(c):
        where = (slice(None), slice(c * wide, (c + 1) * wide))
        return pltpu.make_async_copy(act.at[where], act_h.at[where], sem_o.at[c])

    def activate(first):
        for r in range(0, ROWS, slab):
            rows, at = slice(r, min(r + slab, ROWS)), slice(first, first + cols)
            act[rows, at] = gelu(pre[rows, at].astype(f32)).astype(bf16)

    def multiply(first):
        part = fold3(jnp.dot(reduced[...], act[:, first : first + cols], preferred_element_type=f32))
        for j in range(cols // LANES):
            p_out[first // LANES + j] = part[:, j * LANES : (j + 1) * LANES]

    for c in range(chunks):
        load(c).wait()
        for first in range(c * wide, (c + 1) * wide, cols):
            activate(first)
            if first == 0:
                for copy in small:
                    copy.wait()
                for r in range(0, ROWS, 64):
                    rows = slice(r, min(r + 64, ROWS))
                    scaled[rows, :] = (up[rows, :].astype(f32) * scale[...]).astype(bf16)
                r = lax.dot_general(
                    split3(q[...]), scaled[...], (((1,), (1,)), ((), ())), preferred_element_type=f32
                )
                reduced[...] = split3(fold3(r))
            else:
                multiply(first - cols)
        store(c).start()
    multiply(HID - cols)
    for c in range(chunks):
        store(c).wait()


def front(pre, up, scale, q, chunks=8, cols=256, slab=16):
    return pl.pallas_call(
        functools.partial(front_kernel, chunks, cols, slab),
        in_specs=[pl.BlockSpec(memory_space=pl.ANY)] * 4,
        out_specs=[pl.BlockSpec(memory_space=pltpu.VMEM if i != 1 else pl.ANY) for i in range(4)],
        out_shape=[
            pltpu.VMEM((EVEN, HID), bf16),
            pltpu.HBM((EVEN, HID), bf16),
            pltpu.VMEM((EVEN, WID), bf16),
            pltpu.VMEM((HID // LANES, RANK, LANES), f32),
        ],
        scratch_shapes=[
            pltpu.VMEM((ROWS, HID), bf16),
            pltpu.VMEM((ROWS, WID), bf16),
            pltpu.VMEM((1, WID), f32),
            pltpu.VMEM((RANK, WID), f32),
            pltpu.VMEM((3 * RANK, EVEN), bf16),
            pltpu.SemaphoreType.DMA((chunks,)),
            pltpu.SemaphoreType.DMA((3,)),
            pltpu.SemaphoreType.DMA((chunks,)),
        ],
        compiler_params=pltpu.CompilerParams(vmem_limit_bytes=FRONT_LIMIT),
        cost_estimate=pl.CostEstimate(flops=60 * ROWS * HID, bytes_accessed=10 << 20, transcendentals=ROWS * HID),
        name="front",
    )(pre, up, scale, q)


def project_kernel(act, scaled, p, u_out, keep, send):
    flat = jnp.concatenate([p[j] for j in range(HID // LANES)], axis=1)
    c = lax.dot_general(
        split3(flat), act[...], (((1,), (1,)), ((), ())), preferred_element_type=f32
    )
    u = fold3(jnp.dot(split3(fold3(c)), scaled[...], preferred_element_type=f32))
    core = lax.axis_index("c")
    half = WID // LANES // 2
    for j in range(half):
        low, high = (u[:, k * LANES : (k + 1) * LANES] for k in (j, half + j))
        u_out[j] = low
        u_out[half + j] = high
        keep[j] = jnp.where(core == 0, low, high)
        send[j] = jnp.where(core == 0, high, low)


def project(act, scaled, p):
    n = WID // LANES
    return pl.pallas_call(
        project_kernel,
        in_specs=[pl.BlockSpec(memory_space=pltpu.VMEM)] * 3,
        out_specs=[pl.BlockSpec(memory_space=pltpu.VMEM)] * 3,
        out_shape=[jax.ShapeDtypeStruct((k, RANK, LANES), f32) for k in (n, n // 2, n // 2)],
        compiler_params=pltpu.CompilerParams(vmem_limit_bytes=16 << 20),
        cost_estimate=pl.CostEstimate(flops=48 * ROWS * HID, bytes_accessed=6 << 20, transcendentals=0),
        name="project",
    )(act, scaled, p)


def ortho_kernel(p, u, scaled, basis, inverse, lhs, rhs):
    flat = jnp.concatenate([p[j] for j in range(HID // LANES)], axis=1)
    parts = split3(flat)
    g = lax.dot_general(parts, parts, (((1,), (1,)), ((), ())), preferred_element_type=f32)
    g = fold3(g)
    gram = g[:, 0:RANK] + g[:, RANK : 2 * RANK] + g[:, 2 * RANK : 3 * RANK]
    row = lax.broadcasted_iota(jnp.int32, (RANK, RANK), 0)
    col = lax.broadcasted_iota(jnp.int32, (RANK, RANK), 1)
    inv = jnp.where(row == col, 1.0, 0.0).astype(f32)
    for j in range(RANK):
        root = lax.rsqrt(gram[j : j + 1, j : j + 1])
        gram_row, inv_row = gram[j : j + 1, :] * root, inv[j : j + 1, :] * root
        factor = jnp.where(row[:, 0:1] > j, gram[:, j : j + 1] * root, 0.0)
        gram = jnp.where(row == j, gram_row, gram - factor * gram_row)
        inv = jnp.where(row == j, inv_row, inv - factor * inv_row)
    o = jnp.dot(inv, flat, precision=lax.Precision.HIGHEST, preferred_element_type=f32)
    u_flat = jnp.concatenate([u[j] for j in range(WID // LANES)], axis=1)
    q = jnp.dot(inv, u_flat, precision=lax.Precision.HIGHEST, preferred_element_type=f32)
    basis[...] = o * math.sqrt(HID)
    inverse[...] = inv
    o_hi = (-o).astype(bf16)
    o_lo = (-o - o_hi.astype(f32)).astype(bf16)
    q_hi = q.astype(bf16)
    q_lo = (q - q_hi.astype(f32)).astype(bf16)
    lhs[...] = jnp.concatenate([o_hi, o_hi, o_lo, o_lo], axis=0)
    rhs[0:EVEN, :] = scaled[...]
    rhs[EVEN:AUG, :] = jnp.concatenate([q_hi, q_lo, q_hi, q_lo], axis=0)


def ortho(p, u, scaled):
    return pl.pallas_call(
        ortho_kernel,
        out_shape=[
            jax.ShapeDtypeStruct((RANK, HID), f32),
            jax.ShapeDtypeStruct((RANK, RANK), f32),
            jax.ShapeDtypeStruct((4 * RANK, HID), bf16),
            jax.ShapeDtypeStruct((AUG, WID), bf16),
        ],
        compiler_params=pltpu.CompilerParams(vmem_limit_bytes=8 << 20),
        cost_estimate=pl.CostEstimate(flops=1 << 24, bytes_accessed=1 << 20, transcendentals=0),
        name="ortho",
    )(p, u, scaled)


def residual_kernel(first, blocks, rows, lhs, rhs, act_h, *rest):
    out, mark, held, buf, sem_in, sem_out = rest[-6:]
    mark[...] = jnp.zeros_like(mark)
    contract = (((0,), (0,)), ((), ()))

    def load(b):
        at = slice((first + b) * rows, (first + b + 1) * rows)
        return pltpu.make_async_copy(act_h.at[:, at], held.at[b, 0:EVEN, :], sem_in.at[b])

    def store(b):
        at = slice((first + b) * rows, (first + b + 1) * rows)
        return pltpu.make_async_copy(buf.at[b % 2], out.at[at, :], sem_out.at[b % 2])

    for b in range(blocks):
        load(b).start()
    for b in range(blocks):
        held[b, EVEN:AUG, :] = lhs[:, (first + b) * rows : (first + b + 1) * rows]
    for b in range(blocks):
        load(b).wait()
        if b >= 2:
            store(b - 2).wait()
        buf[b % 2] = lax.dot_general(
            held[b], rhs[...], contract, preferred_element_type=f32
        ).astype(bf16)
        store(b).start()
    for b in range(max(0, blocks - 2), blocks):
        store(b).wait()


def residual_piece(lhs, rhs, act_h, before, first, blocks, rows=512):
    anywhere, vmem = pl.BlockSpec(memory_space=pl.ANY), pl.BlockSpec(memory_space=pltpu.VMEM)
    earlier = [] if before is None else [before]
    return pl.pallas_call(
        functools.partial(residual_kernel, first, blocks, rows),
        in_specs=[vmem, vmem, anywhere] + [anywhere] * len(earlier),
        out_specs=[anywhere, vmem],
        out_shape=[jax.ShapeDtypeStruct((HID, WID), bf16), jax.ShapeDtypeStruct((RANK, LANES), f32)],
        scratch_shapes=[
            pltpu.VMEM((blocks, AUG, rows), bf16),
            pltpu.VMEM((2, rows, WID), bf16),
            pltpu.SemaphoreType.DMA((blocks,)),
            pltpu.SemaphoreType.DMA((2,)),
        ],
        input_output_aliases={3: 0} if earlier else {},
        compiler_params=pltpu.CompilerParams(vmem_limit_bytes=RES_LIMIT),
        cost_estimate=pl.CostEstimate(
            flops=PIECE_FLOPS * blocks, bytes_accessed=(2 << 20) * blocks, transcendentals=0
        ),
        name="residual",
    )(lhs, rhs, act_h, *earlier)


def finish_kernel(inverse, mine, other, q_out, *, devices):
    first = lax.axis_index("c") == 0
    half = WID // LANES // 2
    flat = jnp.concatenate(
        [jnp.where(first, mine[j], other[j]) for j in range(half)]
        + [jnp.where(first, other[j], mine[j]) for j in range(half)],
        axis=1,
    )
    q = jnp.dot(inverse[...], flat, precision=lax.Precision.HIGHEST, preferred_element_type=f32)
    q_out[...] = q * (1.0 / math.sqrt(devices))


def finish(inverse, mine, other, devices):
    return pl.pallas_call(
        functools.partial(finish_kernel, devices=devices),
        out_shape=jax.ShapeDtypeStruct((RANK, WID), f32),
        compiler_params=pltpu.CompilerParams(vmem_limit_bytes=4 << 20),
        name="finish",
    )(inverse, mine, other)


def total(v):
    terms = [v[i] for i in range(v.shape[0])]
    while len(terms) > 1:
        terms = [a + b for a, b in zip(terms[0::2], terms[1::2])]
    return terms[0]


def total_kernel(v, after, out):
    out[...] = total(v)


def total_after(v, after):
    return pl.pallas_call(
        total_kernel,
        in_specs=[pl.BlockSpec(memory_space=pltpu.VMEM)] * 2,
        out_specs=pl.BlockSpec(memory_space=pltpu.VMEM),
        out_shape=jax.ShapeDtypeStruct(v.shape[1:], f32),
        compiler_params=pltpu.CompilerParams(vmem_limit_bytes=4 << 20),
        name="total",
    )(v, after)


def swap(v):
    return lax.ppermute(v, "c", [(0, 1), (1, 0)])


def gather_all_to_all(v, axes, n):
    copies = jnp.broadcast_to(v[None], (n,) + v.shape).reshape((n * v.shape[0],) + v.shape[1:])
    return lax.all_to_all(copies, axes, 0, 0, tiled=True)


def body(pre_act, upstream, layer_scale, initial_q):
    act, act_h, scaled, p_local = front(pre_act, upstream, layer_scale.reshape(1, WID), initial_q)
    with jax.named_scope("sum_p"):
        part = total(lax.all_to_all(p_local, PLANE, 0, 0, tiled=True))
        part = total(gather_all_to_all(part[None], "z", 8))
        p_total = gather_all_to_all(part[None], PLANE, 32)
    u, keep, send = project(act, scaled, p_total)
    basis_out, inverse, lhs, rhs = ortho(p_total, u, scaled)
    early, mark = residual_piece(lhs, rhs, act_h, None, 0, SPLIT)
    residual, last_mark = residual_piece(lhs, rhs, act_h, early, SPLIT, 8 - SPLIT)
    with jax.named_scope("sum_u"):
        t = keep + swap(send)
        t = total_after(gather_all_to_all(t[None], ("x", "y"), 16).reshape(16, 4, RANK, LANES), mark)
        t = total_after(gather_all_to_all(t[None], "z", 8).reshape(8, 4, RANK, LANES), last_mark)
        other = swap(t)
    q_out = finish(inverse, t, other, 256)
    return (basis_out, q_out, residual)


def solution(mesh):
    fine = Mesh(mesh.devices.reshape(8, 4, 4, 2), ("z", "x", "y", "c"))
    split = P(("z", "x", "y", "c"), None)
    return jax.shard_map(
        body, mesh=fine, in_specs=(split, split, P(), P()), out_specs=(P(), P(), split), check_vma=False
    )
```

time: 101 us -> 83.2 us (0.82)
  the two profiles are of different devices: /device:TPU:96 before, /device:TPU:1 now
where the time goes in v2:
time: 83.2 us; the launch traced here: 82.8 us
  blocking collectives  43.7 us (53%)
  Pallas kernels  23.8 us (29%)
  starting transfers between devices  10.5 us (13%)
  waiting for transfers between devices  2.64 us (3%)
  local copies, waits for them, and re-layouts  1.42 us (2%)
    all_to_all x2, blocking collectives, gather_all_to_all(): return lax.all_to_all(copies, axes, 0, 0, tiled=True)  27.6 us
    all_to_all x1, blocking collectives, body(): part = total(lax.all_to_all(p_local, PLANE, 0, 0, tiled=True))  16.1 us
    pallas_call x2, Pallas kernels, residual_piece(): pl.pallas_call(functools.partial(residual_kernel, first, blocks, rows), i...  12.3 us
    all_to_all x2, starting transfers between devices, gather_all_to_all(): return lax.all_to_all(copies, axes, 0, 0, tiled=True)  7.08 us
    pallas_call x1, Pallas kernels, front(): pl.pallas_call(functools.partial(front_kernel, chunks, cols, slab), in_sp...  6.68 us
    ppermute x2, starting transfers between devices, swap(): return lax.ppermute(v, 'c', [(0, 1), (1, 0)])  3.4 us
    pallas_call x1, Pallas kernels, ortho(): pl.pallas_call(ortho_kernel, out_shape=[jax.ShapeDtypeStruct((RANK, HID),...  2.12 us
    pallas_call x1, Pallas kernels, project(): pl.pallas_call(project_kernel, in_specs=[pl.BlockSpec(memory_space=pltpu....  1.94 us
  transfers between devices with their start and end apart: 4, of which 4 were waited for; matrix products, arithmetic and copies ran while one was open for 0% of the time, Pallas kernels for 17%

profile of v2, /device:TPU:1, one launch (start us, length us, event | category | flops | bytes accessed | tf_op | source)
XLA Modules:
  0.0 82.8 jit_solution(6555684754888526042)
XLA Ops:
  0.6 6.7 %front.1 = (bf16[592,4096]{1,0:T(8,128)(2,1)S(1)}, bf16[592,4096]{1,0:T(8,128)(2,1)}, bf16[592,1024]{1,0:T(8,128)(2,1)S(1)}, f32[32,8,128]{2,1,0:T(8,128)S(1)}) custom-call(bf16[588,4096]{1,0:T(8,128)(2,1)} %pre_h.1, bf16[588,1024]{1,0:T(8,128)(2,1)} %up_h.1, f32[1,1024]{1,0:T(1,128)} %bitcast.5, f32[8,1024]{1,0:T(8,128)} %q_h.1), custom_call_target="tpu_custom_call" | custom-call | flops 144506880 | bytes 10485760 | tf_op jit(solution)/shard_map/front/pallas_call | solution.py:95
  7.3 16.1 %all_to_all.25 = f32[32,8,128]{2,1,0:T(8,128)S(1)} all-to-all(f32[32,8,128]{2,1,0:T(8,128)S(1)} %get-tuple-element.18), channel_id=1, replica_groups=mesh['z'=8,'x'=4,'y'=4,'c'=2] {'x','y','c'}, dimensions={0} | all-to-all | bytes 262144 | tf_op jit(solution)/shard_map/sum_p/all_to_all | solution.py:301
  23.4 15.0 %all_to_all.26 = f32[8,8,128]{2,1,0:T(8,128)S(1)} all-to-all(f32[8,8,128]{2,1,0:T(8,128)S(1)} %reshape.267), channel_id=1, replica_groups=mesh['z'=8,'x'=4,'y'=4,'c'=2] {'z'}, dimensions={0} | all-to-all | bytes 65536 | tf_op jit(solution)/shard_map/sum_p/all_to_all | solution.py:295
  38.4 12.6 %all_to_all.27.p = f32[32,8,128]{2,1,0:T(8,128)S(1)} all-to-all(f32[32,8,128]{2,1,0:T(8,128)S(1)} %reshape.268), channel_id=1, replica_groups=mesh['z'=8,'x'=4,'y'=4,'c'=2] {'x','y','c'}, dimensions={0} | all-to-all | bytes 262144 | tf_op jit(solution)/shard_map/sum_p/all_to_all | solution.py:295
  51.0 1.9 %project.1 = (f32[8,8,128]{2,1,0:T(8,128)S(1)}, f32[4,8,128]{2,1,0:T(8,128)S(1)}, f32[4,8,128]{2,1,0:T(8,128)S(1)}) custom-call(bf16[592,4096]{1,0:T(8,128)(2,1)S(1)} %get-tuple-element.19.act, bf16[592,1024]{1,0:T(8,128)(2,1)S(1)} %get-tuple-element.20.scaled, f32[32,8,128]{2,1,0:T(8,128)S(1)} %all_to_all.27.p), custom_call_target="tpu_custom_call" | custom-call | flops 115605504 | bytes 6291456 | tf_op jit(solution)/shard_map/project/pallas_call | solution.py:139
  53.0 0.5 collective-permute-start
  53.5 0.8 %collective-permute-done = f32[4,8,128]{2,1,0:T(8,128)S(1)} collective-permute-done((f32[4,8,128]{2,1,0:T(8,128)S(1)}, f32[4,8,128]{2,1,0:T(8,128)S(1)}, u32[]{:S(2)}, u32[]{:S(2)}) %collective-permute-start) | collective-permute-done | bytes 16416 | tf_op jit(solution)/shard_map/sum_u/ppermute | solution.py:290
  54.3 0.7 reshape.269
  55.0 3.5 %all-to-all-start.3 = ((f32[16,4,8,128]{3,2,1,0:T(8,128)}), f32[16,4,8,128]{3,2,1,0:T(8,128)S(1)}, u32[]{:S(2)}, u32[]{:S(2)}) async-start(f32[16,4,8,128]{3,2,1,0:T(8,128)} %reshape.269), calls=%async_computation.3 | async-start | bytes 524288 | tf_op jit(solution)/shard_map/sum_u/all_to_all | solution.py:295
  58.6 2.1 %ortho.1 = (f32[8,4096]{1,0:T(8,128)}, f32[8,8]{1,0:T(8,128)S(1)}, bf16[32,4096]{1,0:T(8,128)(2,1)S(1)}, bf16[624,1024]{1,0:T(8,128)(2,1)S(1)}) custom-call(f32[32,8,128]{2,1,0:T(8,128)S(1)} %all_to_all.27.p, f32[8,8,128]{2,1,0:T(8,128)S(1)} %get-tuple-element.21.u, bf16[592,1024]{1,0:T(8,128)(2,1)S(1)} %get-tuple-element.20.scaled), custom_call_target="tpu_custom_call" | custom-call | flops 16777216 | bytes 1048576 | tf_op jit(solution)/shard_map/ortho/pallas_call | solution.py:180
  60.7 5.1 %residual.2 = (bf16[4096,1024]{1,0:T(8,128)(2,1)}, f32[8,128]{1,0:T(8,128)S(1)}) custom-call(bf16[32,4096]{1,0:T(8,128)(2,1)S(1)} %get-tuple-element.26.lhs, bf16[624,1024]{1,0:T(8,128)(2,1)S(1)} %get-tuple-element.27.rhs, bf16[592,4096]{1,0:T(8,128)(2,1)} %get-tuple-element.28.act_h), custom_call_target="tpu_custom_call" | custom-call | flops 1849688064 | bytes 6291456 | tf_op jit(solution)/shard_map/residual/pallas_call | solution.py:226
  65.8 0.5 all-to-all-done.3.v
  66.3 0.7 reshape.270
  67.0 3.5 %all-to-all-start.4 = ((f32[8,4,8,128]{3,2,1,0:T(8,128)}), f32[8,4,8,128]{3,2,1,0:T(8,128)S(1)}, u32[]{:S(2)}, u32[]{:S(2)}) async-start(f32[8,4,8,128]{3,2,1,0:T(8,128)} %reshape.270), calls=%async_computation.4 | async-start | bytes 262144 | tf_op jit(solution)/shard_map/sum_u/all_to_all | solution.py:295
  70.5 7.2 %residual.3 = (bf16[4096,1024]{1,0:T(8,128)(2,1)}, f32[8,128]{1,0:T(8,128)S(1)}) custom-call(bf16[32,4096]{1,0:T(8,128)(2,1)S(1)} %get-tuple-element.26.lhs, bf16[624,1024]{1,0:T(8,128)(2,1)S(1)} %get-tuple-element.27.rhs, bf16[592,4096]{1,0:T(8,128)(2,1)} %get-tuple-element.28.act_h, ...), custom_call_target="tpu_custom_call", output_to_operand_aliasing={{0}: (3, {})} | custom-call | flops 3082813440 | bytes 10485760 | tf_op jit(solution)/shard_map/residual/pallas_call | solution.py:226
  77.7 0.5 all-to-all-done.4.v
  78.2 2.9 %collective-permute-start.1 = (f32[4,8,128]{2,1,0:T(8,128)S(1)}, f32[4,8,128]{2,1,0:T(8,128)S(1)}, u32[]{:S(2)}, u32[]{:S(2)}) collective-permute-start(f32[4,8,128]{2,1,0:T(8,128)S(1)} %total.3.mine), channel_id=1, source_target_pairs={{0,1},{1,0},{2,3},{3,2},{4,5},{5,4},{6,7},{7,6},{8,9},{9,8},{10,11... | collective-permute-start | bytes 49160 | tf_op jit(solution)/shard_map/sum_u/ppermute | solution.py:290
  81.1 0.8 %collective-permute-done.1.other = f32[4,8,128]{2,1,0:T(8,128)S(1)} collective-permute-done((f32[4,8,128]{2,1,0:T(8,128)S(1)}, f32[4,8,128]{2,1,0:T(8,128)S(1)}, u32[]{:S(2)}, u32[]{:S(2)}) %collective-permute-start.1) | collective-permute-done | bytes 16416 | tf_op jit(solution)/shard_map/sum_u/ppermute | solution.py:290
  82.0 0.8 finish.1
  (7 shorter events, 0.1 us)
Async XLA Ops:
  53.0 1.3 %collective-permute-start = (f32[4,8,128]{2,1,0:T(8,128)S(1)}, f32[4,8,128]{2,1,0:T(8,128)S(1)}, u32[]{:S(2)}, u32[]{:S(2)}) collective-permute-start(f32[4,8,128]{2,1,0:T(8,128)S(1)} %get-tuple-element.25), channel_id=1, source_target_pairs={{0,1},{1,0},{2,3},{3,2},{4,5},{5,4},{6,7},{7,6},{8,9},{9,8},{10,11... | collective-permute-start | bytes 49160 | tf_op jit(solution)/shard_map/sum_u/ppermute | solution.py:290
  55.0 11.2 %all-to-all-start.3 = ((f32[16,4,8,128]{3,2,1,0:T(8,128)}), f32[16,4,8,128]{3,2,1,0:T(8,128)S(1)}, u32[]{:S(2)}, u32[]{:S(2)}) async-start(f32[16,4,8,128]{3,2,1,0:T(8,128)} %reshape.269), calls=%async_computation.3 | async-start | bytes 524288 | tf_op jit(solution)/shard_map/sum_u/all_to_all | solution.py:295
  67.0 11.2 %all-to-all-start.4 = ((f32[8,4,8,128]{3,2,1,0:T(8,128)}), f32[8,4,8,128]{3,2,1,0:T(8,128)S(1)}, u32[]{:S(2)}, u32[]{:S(2)}) async-start(f32[8,4,8,128]{3,2,1,0:T(8,128)} %reshape.270), calls=%async_computation.4 | async-start | bytes 262144 | tf_op jit(solution)/shard_map/sum_u/all_to_all | solution.py:295
  78.2 3.8 %collective-permute-start.1 = (f32[4,8,128]{2,1,0:T(8,128)S(1)}, f32[4,8,128]{2,1,0:T(8,128)S(1)}, u32[]{:S(2)}, u32[]{:S(2)}) collective-permute-start(f32[4,8,128]{2,1,0:T(8,128)S(1)} %total.3.mine), channel_id=1, source_target_pairs={{0,1},{1,0},{2,3},{3,2},{4,5},{5,4},{6,7},{7,6},{8,9},{9,8},{10,11... | collective-permute-start | bytes 49160 | tf_op jit(solution)/shard_map/sum_u/ppermute | solution.py:290

commit v3 on v2

v3 whole, which is shorter than its diff:
```python
import functools
import math

import jax
import jax.numpy as jnp
from jax import lax
from jax.experimental import pallas as pl
from jax.experimental.pallas import tpu as pltpu
from jax.sharding import Mesh
from jax.sharding import PartitionSpec as P

f32, bf16 = jnp.float32, jnp.bfloat16
ROWS, HID, WID, RANK, LANES = 588, 4096, 1024, 8, 128
EVEN, AUG = 592, 624
FRONT_LIMIT, RES_LIMIT = 52 << 20, 50 << 20
BANDS = ((0, 64), (64, 256), (256, 512), (512, ROWS))
SPANS_A = ((0, 768), (768, 1280))
SPANS_B = ((1280, 1536), (1536, 2304), (2304, 3072), (3072, 3840), (3840, 4096))
PLANE = ("x", "y", "c")


def split3(v):
    a = v.astype(bf16)
    r = v - a.astype(f32)
    b = r.astype(bf16)
    c = (r - b.astype(f32)).astype(bf16)
    return jnp.concatenate([a, b, c], axis=0)


def fold3(v):
    return v[0:RANK] + v[RANK : 2 * RANK] + v[2 * RANK : 3 * RANK]


def gelu(v):
    return 0.5 * v * (1.0 + lax.erf(v * math.sqrt(0.5)))


def front_kernel(
    slab, cols, pre_h, up_h, scale_h, q_h, act, act_h, scaled, p_out, pre, up, scale, q, reduced, sem, sem_s, sem_o
):
    def load(b):
        rows = slice(*BANDS[b])
        return pltpu.make_async_copy(pre_h.at[rows, :], pre.at[rows, :], sem.at[b])

    def store(b):
        first, last = BANDS[b]
        rows = slice(first, EVEN if last == ROWS else last)
        return pltpu.make_async_copy(act.at[rows, :], act_h.at[rows, :], sem_o.at[b])

    small = [
        pltpu.make_async_copy(q_h, q, sem_s.at[0]),
        pltpu.make_async_copy(scale_h, scale, sem_s.at[1]),
        pltpu.make_async_copy(up_h, up, sem_s.at[2]),
    ]
    load(0).start()
    for copy in small:
        copy.start()
    for b in range(1, len(BANDS)):
        load(b).start()
    act[EVEN - 16 : EVEN, :] = jnp.zeros((16, HID), bf16)
    scaled[EVEN - 16 : EVEN, :] = jnp.zeros((16, WID), bf16)
    for b, (first, last) in enumerate(BANDS):
        load(b).wait()
        for left in range(0, HID, cols):
            for r in range(first, last, slab):
                rows, at = slice(r, min(r + slab, last)), slice(left, left + cols)
                act[rows, at] = gelu(pre[rows, at].astype(f32)).astype(bf16)
        store(b).start()
    for copy in small:
        copy.wait()
    for r in range(0, ROWS, 64):
        rows = slice(r, min(r + 64, ROWS))
        scaled[rows, :] = (up[rows, :].astype(f32) * scale[...]).astype(bf16)
    r = lax.dot_general(
        split3(q[...]), scaled[...], (((1,), (1,)), ((), ())), preferred_element_type=f32
    )
    reduced[...] = split3(fold3(r))
    for left in range(0, HID, cols):
        part = fold3(jnp.dot(reduced[...], act[:, left : left + cols], preferred_element_type=f32))
        for j in range(cols // LANES):
            p_out[left // LANES + j] = part[:, j * LANES : (j + 1) * LANES]
    for b in range(len(BANDS)):
        store(b).wait()


def front(pre, up, scale, q, slab=16, cols=512):
    return pl.pallas_call(
        functools.partial(front_kernel, slab, cols),
        in_specs=[pl.BlockSpec(memory_space=pl.ANY)] * 4,
        out_specs=[pl.BlockSpec(memory_space=pltpu.VMEM if i != 1 else pl.ANY) for i in range(4)],
        out_shape=[
            pltpu.VMEM((EVEN, HID), bf16),
            pltpu.HBM((EVEN, HID), bf16),
            pltpu.VMEM((EVEN, WID), bf16),
            pltpu.VMEM((HID // LANES, RANK, LANES), f32),
        ],
        scratch_shapes=[
            pltpu.VMEM((ROWS, HID), bf16),
            pltpu.VMEM((ROWS, WID), bf16),
            pltpu.VMEM((1, WID), f32),
            pltpu.VMEM((RANK, WID), f32),
            pltpu.VMEM((3 * RANK, EVEN), bf16),
            pltpu.SemaphoreType.DMA((len(BANDS),)),
            pltpu.SemaphoreType.DMA((3,)),
            pltpu.SemaphoreType.DMA((len(BANDS),)),
        ],
        compiler_params=pltpu.CompilerParams(vmem_limit_bytes=FRONT_LIMIT),
        cost_estimate=pl.CostEstimate(flops=60 * ROWS * HID, bytes_accessed=10 << 20, transcendentals=ROWS * HID),
        name="front",
    )(pre, up, scale, q)


def project_kernel(act, scaled, p, u_out, keep, send):
    flat = jnp.concatenate([p[j] for j in range(HID // LANES)], axis=1)
    c = lax.dot_general(
        split3(flat), act[...], (((1,), (1,)), ((), ())), preferred_element_type=f32
    )
    u = fold3(jnp.dot(split3(fold3(c)), scaled[...], preferred_element_type=f32))
    core = lax.axis_index("c")
    half = WID // LANES // 2
    for j in range(half):
        low, high = (u[:, k * LANES : (k + 1) * LANES] for k in (j, half + j))
        u_out[j] = low
        u_out[half + j] = high
        keep[j] = jnp.where(core == 0, low, high)
        send[j] = jnp.where(core == 0, high, low)


def project(act, scaled, p):
    n = WID // LANES
    return pl.pallas_call(
        project_kernel,
        in_specs=[pl.BlockSpec(memory_space=pltpu.VMEM)] * 3,
        out_specs=[pl.BlockSpec(memory_space=pltpu.VMEM)] * 3,
        out_shape=[jax.ShapeDtypeStruct((k, RANK, LANES), f32) for k in (n, n // 2, n // 2)],
        compiler_params=pltpu.CompilerParams(vmem_limit_bytes=16 << 20),
        cost_estimate=pl.CostEstimate(flops=48 * ROWS * HID, bytes_accessed=6 << 20, transcendentals=0),
        name="project",
    )(act, scaled, p)


def ortho_kernel(p, u, scaled, act_h, basis, inverse, lhs, rhs, out, held, buf, sem_in, sem_out):
    finish_rows = residual_rows(SPANS_A, lhs, rhs, act_h, out, held, buf, sem_in, sem_out)
    flat = jnp.concatenate([p[j] for j in range(HID // LANES)], axis=1)
    parts = split3(flat)
    g = lax.dot_general(parts, parts, (((1,), (1,)), ((), ())), preferred_element_type=f32)
    g = fold3(g)
    gram = g[:, 0:RANK] + g[:, RANK : 2 * RANK] + g[:, 2 * RANK : 3 * RANK]
    row = lax.broadcasted_iota(jnp.int32, (RANK, RANK), 0)
    col = lax.broadcasted_iota(jnp.int32, (RANK, RANK), 1)
    inv = jnp.where(row == col, 1.0, 0.0).astype(f32)
    for j in range(RANK):
        root = lax.rsqrt(gram[j : j + 1, j : j + 1])
        gram_row, inv_row = gram[j : j + 1, :] * root, inv[j : j + 1, :] * root
        factor = jnp.where(row[:, 0:1] > j, gram[:, j : j + 1] * root, 0.0)
        gram = jnp.where(row == j, gram_row, gram - factor * gram_row)
        inv = jnp.where(row == j, inv_row, inv - factor * inv_row)
    o = jnp.dot(inv, flat, precision=lax.Precision.HIGHEST, preferred_element_type=f32)
    u_flat = jnp.concatenate([u[j] for j in range(WID // LANES)], axis=1)
    q = jnp.dot(inv, u_flat, precision=lax.Precision.HIGHEST, preferred_element_type=f32)
    basis[...] = o * math.sqrt(HID)
    inverse[...] = inv
    o_hi = (-o).astype(bf16)
    o_lo = (-o - o_hi.astype(f32)).astype(bf16)
    q_hi = q.astype(bf16)
    q_lo = (q - q_hi.astype(f32)).astype(bf16)
    lhs[...] = jnp.concatenate([o_hi, o_hi, o_lo, o_lo], axis=0)
    rhs[0:EVEN, :] = scaled[...]
    rhs[EVEN:AUG, :] = jnp.concatenate([q_hi, q_lo, q_hi, q_lo], axis=0)
    finish_rows()


def residual_rows(spans, lhs, rhs, act_h, out, held, buf, sem_in, sem_out):
    base, end = spans[0][0], spans[-1][1]

    def load(b):
        low, high = spans[b]
        return pltpu.make_async_copy(
            act_h.at[:, low:high], held.at[0:EVEN, low - base : high - base], sem_in.at[b]
        )

    def store(b):
        low, high = spans[b]
        return pltpu.make_async_copy(
            buf.at[b % 2, 0 : high - low, :], out.at[low:high, :], sem_out.at[b % 2]
        )

    for b in range(len(spans)):
        load(b).start()

    def compute():
        held[EVEN:AUG, :] = lhs[:, base:end]
        for b, (low, high) in enumerate(spans):
            load(b).wait()
            if b >= 2:
                store(b - 2).wait()
            buf[b % 2, 0 : high - low, :] = lax.dot_general(
                held[:, low - base : high - base],
                rhs[...],
                (((0,), (0,)), ((), ())),
                preferred_element_type=f32,
            ).astype(bf16)
            store(b).start()
        for b in range(max(0, len(spans) - 2), len(spans)):
            store(b).wait()

    return compute


def residual_scratch(spans):
    return [
        pltpu.VMEM((AUG, spans[-1][1] - spans[0][0]), bf16),
        pltpu.VMEM((2, max(high - low for low, high in spans), WID), bf16),
        pltpu.SemaphoreType.DMA((len(spans),)),
        pltpu.SemaphoreType.DMA((2,)),
    ]


def ortho(p, u, scaled, act_h):
    anywhere, vmem = pl.BlockSpec(memory_space=pl.ANY), pl.BlockSpec(memory_space=pltpu.VMEM)
    return pl.pallas_call(
        ortho_kernel,
        in_specs=[vmem, vmem, vmem, anywhere],
        out_specs=[vmem, vmem, vmem, vmem, anywhere],
        out_shape=[
            jax.ShapeDtypeStruct((RANK, HID), f32),
            jax.ShapeDtypeStruct((RANK, RANK), f32),
            jax.ShapeDtypeStruct((4 * RANK, HID), bf16),
            jax.ShapeDtypeStruct((AUG, WID), bf16),
            jax.ShapeDtypeStruct((HID, WID), bf16),
        ],
        scratch_shapes=residual_scratch(SPANS_A),
        compiler_params=pltpu.CompilerParams(vmem_limit_bytes=RES_LIMIT),
        cost_estimate=pl.CostEstimate(
            flops=2 * ROWS * HID * WID // 2, bytes_accessed=6 << 20, transcendentals=0
        ),
        name="ortho",
    )(p, u, scaled, act_h)


def residual_kernel(lhs, rhs, act_h, before, out, mark, held, buf, sem_in, sem_out):
    mark[...] = jnp.zeros_like(mark)
    residual_rows(SPANS_B, lhs, rhs, act_h, out, held, buf, sem_in, sem_out)()


def residual_of(lhs, rhs, act_h, before):
    anywhere, vmem = pl.BlockSpec(memory_space=pl.ANY), pl.BlockSpec(memory_space=pltpu.VMEM)
    return pl.pallas_call(
        residual_kernel,
        in_specs=[vmem, vmem, anywhere, anywhere],
        out_specs=[anywhere, vmem],
        out_shape=[jax.ShapeDtypeStruct((HID, WID), bf16), jax.ShapeDtypeStruct((RANK, LANES), f32)],
        scratch_shapes=residual_scratch(SPANS_B),
        input_output_aliases={3: 0},
        compiler_params=pltpu.CompilerParams(vmem_limit_bytes=RES_LIMIT),
        cost_estimate=pl.CostEstimate(flops=2 * ROWS * HID * WID, bytes_accessed=14 << 20, transcendentals=0),
        name="residual",
    )(lhs, rhs, act_h, before)


def finish_kernel(inverse, u, after, q_out, *, devices):
    parts = [total(u[:, core]) for core in range(2)]
    flat = jnp.concatenate([part[j] for part in parts for j in range(part.shape[0])], axis=1)
    q = jnp.dot(inverse[...], flat, precision=lax.Precision.HIGHEST, preferred_element_type=f32)
    q_out[...] = q * (1.0 / math.sqrt(devices))


def finish(inverse, u, after, devices):
    return pl.pallas_call(
        functools.partial(finish_kernel, devices=devices),
        in_specs=[pl.BlockSpec(memory_space=pltpu.VMEM)] * 3,
        out_specs=pl.BlockSpec(memory_space=pltpu.VMEM),
        out_shape=jax.ShapeDtypeStruct((RANK, WID), f32),
        compiler_params=pltpu.CompilerParams(vmem_limit_bytes=4 << 20),
        name="finish",
    )(inverse, u, after)


def total(v):
    terms = [v[i] for i in range(v.shape[0])]
    while len(terms) > 1:
        terms = [a + b for a, b in zip(terms[0::2], terms[1::2])]
    return terms[0]


def spread_kernel(v, after, out):
    whole = total(v)
    for i in range(out.shape[0]):
        out[i] = whole


def spread(v, after, n):
    return pl.pallas_call(
        spread_kernel,
        in_specs=[pl.BlockSpec(memory_space=pltpu.VMEM)] * 2,
        out_specs=pl.BlockSpec(memory_space=pltpu.VMEM),
        out_shape=pltpu.VMEM((n,) + v.shape[1:], f32),
        compiler_params=pltpu.CompilerParams(vmem_limit_bytes=4 << 20),
        name="spread",
    )(v, after)


def add_spread_kernel(a, b, out):
    whole = a[...] + b[...]
    for i in range(out.shape[0]):
        out[i] = whole


def add_spread(a, b, n):
    return pl.pallas_call(
        add_spread_kernel,
        in_specs=[pl.BlockSpec(memory_space=pltpu.VMEM)] * 2,
        out_specs=pl.BlockSpec(memory_space=pltpu.VMEM),
        out_shape=pltpu.VMEM((n,) + a.shape, f32),
        compiler_params=pltpu.CompilerParams(vmem_limit_bytes=4 << 20),
        name="add_spread",
    )(a, b)


def swap(v):
    return lax.ppermute(v, "c", [(0, 1), (1, 0)])


def gather_all_to_all(v, axes, n):
    copies = jnp.broadcast_to(v[None], (n,) + v.shape).reshape((n * v.shape[0],) + v.shape[1:])
    return lax.all_to_all(copies, axes, 0, 0, tiled=True)


def body(pre_act, upstream, layer_scale, initial_q):
    act, act_h, scaled, p_local = front(pre_act, upstream, layer_scale.reshape(1, WID), initial_q)
    with jax.named_scope("sum_p"):
        part = total(lax.all_to_all(p_local, PLANE, 0, 0, tiled=True))
        part = total(gather_all_to_all(part[None], "z", 8))
        p_total = gather_all_to_all(part[None], PLANE, 32)
    u, keep, send = project(act, scaled, p_total)
    basis_out, inverse, lhs, rhs, early = ortho(p_total, u, scaled, act_h)
    residual, mark = residual_of(lhs, rhs, act_h, early)
    with jax.named_scope("sum_u"):
        t = add_spread(keep, swap(send), 16)
        t = lax.all_to_all(t, ("x", "y"), 0, 0, tiled=True)
        t = spread(t, inverse, 16)
        t = lax.all_to_all(t, ("z", "c"), 0, 0, tiled=True)
    q_out = finish(inverse, t.reshape((8, 2) + t.shape[1:]), mark, 256)
    return (basis_out, q_out, residual)


def solution(mesh):
    fine = Mesh(mesh.devices.reshape(8, 4, 4, 2), ("z", "x", "y", "c"))
    split = P(("z", "x", "y", "c"), None)
    return jax.shard_map(
        body, mesh=fine, in_specs=(split, split, P(), P()), out_specs=(P(), P(), split), check_vma=False
    )
```

time: 83.2 us -> 83.5 us (level)
  waiting for transfers between devices: 2.64 us -> 6.87 us
  starting transfers between devices: 10.5 us -> 9.03 us
  local copies, waits for them, and re-layouts: 1.42 us -> 0.02 us
  Pallas kernels: 23.8 us -> 22.8 us
    all_to_all x2, waiting for transfers between devices: 0.97 us -> 6.03 us  [the longest x1 4.58 us: body(): t = lax.all_to_all(t, ('z', 'c'), 0, 0, tiled=True)]
    ppermute x2 -> x1, starting transfers between devices: 3.4 us -> 0.48 us  [swap(): return lax.ppermute(v, 'c', [(0, 1), (1, 0)])]
    all_to_all x2, starting transfers between devices: 7.08 us -> 8.55 us  [the longest x1 5.02 us: body(): t = lax.all_to_all(t, ('z', 'c'), 0, 0, tiled=True)]
    reshape x4 -> x2, local copies, waits for them, and re-layouts: 1.42 us -> 0.02 us  [gather_all_to_all(): jnp.broadcast_to(v[None], (n,) + v.shape)]
    pallas_call x7 -> x6, Pallas kernels: 21.9 us -> 20.8 us  [the longest x1 7.29 us: residual_of(): pl.pallas_call(residual_kernel, in_specs=[vmem, vmem, anywhere, anywhere]...]
    ppermute x2 -> x1, waiting for transfers between devices: 1.68 us -> 0.84 us  [swap(): return lax.ppermute(v, 'c', [(0, 1), (1, 0)])]
  transfers between devices with their start and end apart: 4 -> 3, of which waited for: 4 -> 3; matrix products, arithmetic and copies ran while one was open for 0% -> 0% of each run, Pallas kernels for 17% -> 16%
where the time goes in v3:
time: 83.5 us; the launch traced here: 83.1 us
  blocking collectives  43.7 us (52%)
  Pallas kernels  22.8 us (27%)
  starting transfers between devices  9.03 us (11%)
  waiting for transfers between devices  6.87 us (8%)
    all_to_all x2, blocking collectives, gather_all_to_all(): return lax.all_to_all(copies, axes, 0, 0, tiled=True)  27.6 us
    all_to_all x1, blocking collectives, body(): part = total(lax.all_to_all(p_local, PLANE, 0, 0, tiled=True))  16.1 us
    pallas_call x1, Pallas kernels, residual_of(): pl.pallas_call(residual_kernel, in_specs=[vmem, vmem, anywhere, anywhere]...  7.29 us
    pallas_call x1, Pallas kernels, ortho(): pl.pallas_call(ortho_kernel, in_specs=[vmem, vmem, vmem, anywhere], out_s...  6.24 us
    all_to_all x1, starting transfers between devices, body(): t = lax.all_to_all(t, ('z', 'c'), 0, 0, tiled=True)  5.02 us
    pallas_call x1, Pallas kernels, front(): pl.pallas_call(functools.partial(front_kernel, slab, cols), in_specs=[pl....  5.01 us
    all_to_all x1, waiting for transfers between devices, body(): t = lax.all_to_all(t, ('z', 'c'), 0, 0, tiled=True)  4.58 us
    all_to_all x1, starting transfers between devices, body(): t = lax.all_to_all(t, ('x', 'y'), 0, 0, tiled=True)  3.53 us
  transfers between devices with their start and end apart: 3, of which 3 were waited for; matrix products, arithmetic and copies ran while one was open for 0% of the time, Pallas kernels for 16%

profile of v3, /device:TPU:1, one launch (start us, length us, event | category | flops | bytes accessed | tf_op | source)
XLA Modules:
  0.0 83.1 jit_solution(12464648321219859939)
XLA Ops:
  0.6 5.0 %front.1 = (bf16[592,4096]{1,0:T(8,128)(2,1)S(1)}, bf16[592,4096]{1,0:T(8,128)(2,1)}, bf16[592,1024]{1,0:T(8,128)(2,1)S(1)}, f32[32,8,128]{2,1,0:T(8,128)S(1)}) custom-call(bf16[588,4096]{1,0:T(8,128)(2,1)} %pre_h.1, bf16[588,1024]{1,0:T(8,128)(2,1)} %up_h.1, f32[1,1024]{1,0:T(1,128)} %bitcast.7, f32[8,1024]{1,0:T(8,128)} %q_h.1), custom_call_target="tpu_custom_call" | custom-call | flops 144506880 | bytes 10485760 | tf_op jit(solution)/shard_map/front/pallas_call | solution.py:87
  5.7 16.1 %all_to_all.25 = f32[32,8,128]{2,1,0:T(8,128)S(1)} all-to-all(f32[32,8,128]{2,1,0:T(8,128)S(1)} %get-tuple-element.17), channel_id=1, replica_groups=mesh['z'=8,'x'=4,'y'=4,'c'=2] {'x','y','c'}, dimensions={0} | all-to-all | bytes 262144 | tf_op jit(solution)/shard_map/sum_p/all_to_all | solution.py:332
  21.8 15.0 %all_to_all.26 = f32[8,8,128]{2,1,0:T(8,128)S(1)} all-to-all(f32[8,8,128]{2,1,0:T(8,128)S(1)} %reshape.258), channel_id=1, replica_groups=mesh['z'=8,'x'=4,'y'=4,'c'=2] {'z'}, dimensions={0} | all-to-all | bytes 65536 | tf_op jit(solution)/shard_map/sum_p/all_to_all | solution.py:326
  36.7 12.6 %all_to_all.27.p = f32[32,8,128]{2,1,0:T(8,128)S(1)} all-to-all(f32[32,8,128]{2,1,0:T(8,128)S(1)} %reshape.259), channel_id=1, replica_groups=mesh['z'=8,'x'=4,'y'=4,'c'=2] {'x','y','c'}, dimensions={0} | all-to-all | bytes 262144 | tf_op jit(solution)/shard_map/sum_p/all_to_all | solution.py:326
  49.4 1.9 %project.1 = (f32[8,8,128]{2,1,0:T(8,128)S(1)}, f32[4,8,128]{2,1,0:T(8,128)S(1)}, f32[4,8,128]{2,1,0:T(8,128)S(1)}) custom-call(bf16[592,4096]{1,0:T(8,128)(2,1)S(1)} %get-tuple-element.18.act, bf16[592,1024]{1,0:T(8,128)(2,1)S(1)} %get-tuple-element.19.scaled, f32[32,8,128]{2,1,0:T(8,128)S(1)} %all_to_all.27.p), custom_call_target="tpu_custom_call" | custom-call | flops 115605504 | bytes 6291456 | tf_op jit(solution)/shard_map/project/pallas_call | solution.py:131
  51.3 0.5 collective-permute-start
  51.8 0.8 %collective-permute-done.b = f32[4,8,128]{2,1,0:T(8,128)S(1)} collective-permute-done((f32[4,8,128]{2,1,0:T(8,128)S(1)}, f32[4,8,128]{2,1,0:T(8,128)S(1)}, u32[]{:S(2)}, u32[]{:S(2)}) %collective-permute-start) | collective-permute-done | bytes 16416 | tf_op jit(solution)/shard_map/sum_u/ppermute | solution.py:321
  52.6 0.7 add_spread.1
  53.4 3.5 %all-to-all-start.3 = ((f32[16,4,8,128]{3,2,1,0:T(8,128)}), f32[16,4,8,128]{3,2,1,0:T(8,128)S(1)}, u32[]{:S(2)}, u32[]{:S(2)}) async-start(f32[16,4,8,128]{3,2,1,0:T(8,128)} %add_spread.1), calls=%async_computation.3 | async-start | bytes 524288 | tf_op jit(solution)/shard_map/sum_u/all_to_all | solution.py:340
  56.9 6.2 %ortho.1 = (f32[8,4096]{1,0:T(8,128)}, f32[8,8]{1,0:T(8,128)S(1)}, bf16[32,4096]{1,0:T(8,128)(2,1)S(1)}, bf16[624,1024]{1,0:T(8,128)(2,1)S(1)}, bf16[4096,1024]{1,0:T(8,128)(2,1)}) custom-call(f32[32,8,128]{2,1,0:T(8,128)S(1)} %all_to_all.27.p, f32[8,8,128]{2,1,0:T(8,128)S(1)} %get-tuple-element.20.u, bf16[592,1024]{1,0:T(8,128)(2,1)S(1)} %get-tuple-element.19.scaled, ...), custom_call_target="tpu_custom_call" | custom-call | flops 2466250752 | bytes 6291456 | tf_op jit(solution)/shard_map/ortho/pallas_call | solution.py:221
  63.2 1.5 %all-to-all-done.3.v = f32[16,4,8,128]{3,2,1,0:T(8,128)S(1)} async-done(((f32[16,4,8,128]{3,2,1,0:T(8,128)}), f32[16,4,8,128]{3,2,1,0:T(8,128)S(1)}, u32[]{:S(2)}, u32[]{:S(2)}) %all-to-all-start.3) | async-done | bytes 262176 | tf_op jit(solution)/shard_map/sum_u/all_to_all | solution.py:340
  64.6 0.7 spread.1
  65.4 5.0 %all-to-all-start.4 = ((f32[16,4,8,128]{3,2,1,0:T(8,128)}), f32[16,4,8,128]{3,2,1,0:T(8,128)S(1)}, u32[]{:S(2)}, u32[]{:S(2)}) async-start(f32[16,4,8,128]{3,2,1,0:T(8,128)} %spread.1), calls=%async_computation.4 | async-start | bytes 524288 | tf_op jit(solution)/shard_map/sum_u/all_to_all | solution.py:342
  70.4 7.3 %residual.1 = (bf16[4096,1024]{1,0:T(8,128)(2,1)}, f32[8,128]{1,0:T(8,128)S(1)}) custom-call(bf16[32,4096]{1,0:T(8,128)(2,1)S(1)} %get-tuple-element.26.lhs, bf16[624,1024]{1,0:T(8,128)(2,1)S(1)} %get-tuple-element.27.rhs, bf16[592,4096]{1,0:T(8,128)(2,1)} %get-tuple-element.21.act_h, ...), custom_call_target="tpu_custom_call", output_to_operand_aliasing={{0}: (3, {})} | custom-call | flops 4932501504 | bytes 14680064 | tf_op jit(solution)/shard_map/residual/pallas_call | solution.py:248
  77.7 4.6 %all-to-all-done.4 = f32[16,4,8,128]{3,2,1,0:T(8,128)S(1)} async-done(((f32[16,4,8,128]{3,2,1,0:T(8,128)}), f32[16,4,8,128]{3,2,1,0:T(8,128)S(1)}, u32[]{:S(2)}, u32[]{:S(2)}) %all-to-all-start.4) | async-done | bytes 262176 | tf_op jit(solution)/shard_map/sum_u/all_to_all | solution.py:342
  82.3 0.8 finish.1
  (4 shorter events, 0.0 us)
Async XLA Ops:
  51.3 1.3 %collective-permute-start = (f32[4,8,128]{2,1,0:T(8,128)S(1)}, f32[4,8,128]{2,1,0:T(8,128)S(1)}, u32[]{:S(2)}, u32[]{:S(2)}) collective-permute-start(f32[4,8,128]{2,1,0:T(8,128)S(1)} %get-tuple-element.25), channel_id=1, source_target_pairs={{0,1},{1,0},{2,3},{3,2},{4,5},{5,4},{6,7},{7,6},{8,9},{9,8},{10,11... | collective-permute-start | bytes 49160 | tf_op jit(solution)/shard_map/sum_u/ppermute | solution.py:321
  53.4 11.2 %all-to-all-start.3 = ((f32[16,4,8,128]{3,2,1,0:T(8,128)}), f32[16,4,8,128]{3,2,1,0:T(8,128)S(1)}, u32[]{:S(2)}, u32[]{:S(2)}) async-start(f32[16,4,8,128]{3,2,1,0:T(8,128)} %add_spread.1), calls=%async_computation.3 | async-start | bytes 524288 | tf_op jit(solution)/shard_map/sum_u/all_to_all | solution.py:340
  65.4 16.9 %all-to-all-start.4 = ((f32[16,4,8,128]{3,2,1,0:T(8,128)}), f32[16,4,8,128]{3,2,1,0:T(8,128)S(1)}, u32[]{:S(2)}, u32[]{:S(2)}) async-start(f32[16,4,8,128]{3,2,1,0:T(8,128)} %spread.1), calls=%async_computation.4 | async-start | bytes 524288 | tf_op jit(solution)/shard_map/sum_u/all_to_all | solution.py:342

commit v4 on v3

--- a/solution.py
+++ b/solution.py
@@ -258,14 +258,19 @@
     )(lhs, rhs, act_h, before)
 
 
-def finish_kernel(inverse, u, after, q_out, *, devices):
-    parts = [total(u[:, core]) for core in range(2)]
-    flat = jnp.concatenate([part[j] for part in parts for j in range(part.shape[0])], axis=1)
+def finish_kernel(inverse, mine, other, q_out, *, devices):
+    first = lax.axis_index("c") == 0
+    half = WID // LANES // 2
+    flat = jnp.concatenate(
+        [jnp.where(first, mine[j], other[j]) for j in range(half)]
+        + [jnp.where(first, other[j], mine[j]) for j in range(half)],
+        axis=1,
+    )
     q = jnp.dot(inverse[...], flat, precision=lax.Precision.HIGHEST, preferred_element_type=f32)
     q_out[...] = q * (1.0 / math.sqrt(devices))
 
 
-def finish(inverse, u, after, devices):
+def finish(inverse, mine, other, devices):
     return pl.pallas_call(
         functools.partial(finish_kernel, devices=devices),
         in_specs=[pl.BlockSpec(memory_space=pltpu.VMEM)] * 3,
@@ -273,7 +278,7 @@
         out_shape=jax.ShapeDtypeStruct((RANK, WID), f32),
         compiler_params=pltpu.CompilerParams(vmem_limit_bytes=4 << 20),
         name="finish",
-    )(inverse, u, after)
+    )(inverse, mine, other)
 
 
 def total(v):
@@ -281,6 +286,21 @@
     while len(terms) > 1:
         terms = [a + b for a, b in zip(terms[0::2], terms[1::2])]
     return terms[0]
+
+
+def total_kernel(v, after, out):
+    out[...] = total(v)
+
+
+def total_after(v, after):
+    return pl.pallas_call(
+        total_kernel,
+        in_specs=[pl.BlockSpec(memory_space=pltpu.VMEM)] * 2,
+        out_specs=pl.BlockSpec(memory_space=pltpu.VMEM),
+        out_shape=jax.ShapeDtypeStruct(v.shape[1:], f32),
+        compiler_params=pltpu.CompilerParams(vmem_limit_bytes=4 << 20),
+        name="total",
+    )(v, after)
 
 
 def spread_kernel(v, after, out):
@@ -338,9 +358,10 @@
     with jax.named_scope("sum_u"):
         t = add_spread(keep, swap(send), 16)
         t = lax.all_to_all(t, ("x", "y"), 0, 0, tiled=True)
-        t = spread(t, inverse, 16)
-        t = lax.all_to_all(t, ("z", "c"), 0, 0, tiled=True)
-    q_out = finish(inverse, t.reshape((8, 2) + t.shape[1:]), mark, 256)
+        t = spread(t, inverse, 8)
+        mine = total_after(lax.all_to_all(t, "z", 0, 0, tiled=True), mark)
+        other = swap(mine)
+    q_out = finish(inverse, mine, other, 256)
     return (basis_out, q_out, residual)
 
 

time: 83.5 us -> 81.5 us (0.976)
  waiting for transfers between devices: 6.87 us -> 3.5 us
  starting transfers between devices: 9.03 us -> 10.5 us
    all_to_all x1, waiting for transfers between devices: 4.58 us -> 0.37 us  [body(): mine = total_after(lax.all_to_all(t, 'z', 0, 0, tiled=True), mark)]
    ppermute x1 -> x2, starting transfers between devices: 0.48 us -> 3.4 us  [swap(): return lax.ppermute(v, 'c', [(0, 1), (1, 0)])]
    all_to_all x1, starting transfers between devices: 5.02 us -> 3.55 us  [body(): mine = total_after(lax.all_to_all(t, 'z', 0, 0, tiled=True), mark)]
    ppermute x1 -> x2, waiting for transfers between devices: 0.84 us -> 1.68 us  [swap(): return lax.ppermute(v, 'c', [(0, 1), (1, 0)])]
  transfers between devices with their start and end apart: 3 -> 4, of which waited for: 3 -> 4; matrix products, arithmetic and copies ran while one was open for 0% -> 0% of each run, Pallas kernels for 16% -> 17%
where the time goes in v4:
time: 81.5 us; the launch traced here: 81.1 us
  blocking collectives  43.7 us (54%)
  Pallas kernels  22.7 us (28%)
  starting transfers between devices  10.5 us (13%)
  waiting for transfers between devices  3.5 us (4%)
    all_to_all x2, blocking collectives, gather_all_to_all(): return lax.all_to_all(copies, axes, 0, 0, tiled=True)  27.6 us
    all_to_all x1, blocking collectives, body(): part = total(lax.all_to_all(p_local, PLANE, 0, 0, tiled=True))  16.1 us
    pallas_call x1, Pallas kernels, residual_of(): pl.pallas_call(residual_kernel, in_specs=[vmem, vmem, anywhere, anywhere]...  7.29 us
    pallas_call x1, Pallas kernels, ortho(): pl.pallas_call(ortho_kernel, in_specs=[vmem, vmem, vmem, anywhere], out_s...  6.24 us
    pallas_call x1, Pallas kernels, front(): pl.pallas_call(functools.partial(front_kernel, slab, cols), in_specs=[pl....  5.01 us
    all_to_all x1, starting transfers between devices, body(): mine = total_after(lax.all_to_all(t, 'z', 0, 0, tiled=True), mark)  3.55 us
    all_to_all x1, starting transfers between devices, body(): t = lax.all_to_all(t, ('x', 'y'), 0, 0, tiled=True)  3.53 us
    ppermute x2, starting transfers between devices, swap(): return lax.ppermute(v, 'c', [(0, 1), (1, 0)])  3.4 us
  transfers between devices with their start and end apart: 4, of which 4 were waited for; matrix products, arithmetic and copies ran while one was open for 0% of the time, Pallas kernels for 17%

profile of v4, /device:TPU:1, one launch (start us, length us, event | category | flops | bytes accessed | tf_op | source)
XLA Modules:
  0.0 81.1 jit_solution(7936637335067258776)
XLA Ops:
  0.6 5.0 %front.1 = (bf16[592,4096]{1,0:T(8,128)(2,1)S(1)}, bf16[592,4096]{1,0:T(8,128)(2,1)}, bf16[592,1024]{1,0:T(8,128)(2,1)S(1)}, f32[32,8,128]{2,1,0:T(8,128)S(1)}) custom-call(bf16[588,4096]{1,0:T(8,128)(2,1)} %pre_h.1, bf16[588,1024]{1,0:T(8,128)(2,1)} %up_h.1, f32[1,1024]{1,0:T(1,128)} %bitcast.5, f32[8,1024]{1,0:T(8,128)} %q_h.1), custom_call_target="tpu_custom_call" | custom-call | flops 144506880 | bytes 10485760 | tf_op jit(solution)/shard_map/front/pallas_call | solution.py:87
  5.7 16.1 %all_to_all.25 = f32[32,8,128]{2,1,0:T(8,128)S(1)} all-to-all(f32[32,8,128]{2,1,0:T(8,128)S(1)} %get-tuple-element.17), channel_id=1, replica_groups=mesh['z'=8,'x'=4,'y'=4,'c'=2] {'x','y','c'}, dimensions={0} | all-to-all | bytes 262144 | tf_op jit(solution)/shard_map/sum_p/all_to_all | solution.py:352
  21.8 15.0 %all_to_all.26 = f32[8,8,128]{2,1,0:T(8,128)S(1)} all-to-all(f32[8,8,128]{2,1,0:T(8,128)S(1)} %reshape.255), channel_id=1, replica_groups=mesh['z'=8,'x'=4,'y'=4,'c'=2] {'z'}, dimensions={0} | all-to-all | bytes 65536 | tf_op jit(solution)/shard_map/sum_p/all_to_all | solution.py:346
  36.7 12.6 %all_to_all.27.p = f32[32,8,128]{2,1,0:T(8,128)S(1)} all-to-all(f32[32,8,128]{2,1,0:T(8,128)S(1)} %reshape.256), channel_id=1, replica_groups=mesh['z'=8,'x'=4,'y'=4,'c'=2] {'x','y','c'}, dimensions={0} | all-to-all | bytes 262144 | tf_op jit(solution)/shard_map/sum_p/all_to_all | solution.py:346
  49.4 1.9 %project.1 = (f32[8,8,128]{2,1,0:T(8,128)S(1)}, f32[4,8,128]{2,1,0:T(8,128)S(1)}, f32[4,8,128]{2,1,0:T(8,128)S(1)}) custom-call(bf16[592,4096]{1,0:T(8,128)(2,1)S(1)} %get-tuple-element.18.act, bf16[592,1024]{1,0:T(8,128)(2,1)S(1)} %get-tuple-element.19.scaled, f32[32,8,128]{2,1,0:T(8,128)S(1)} %all_to_all.27.p), custom_call_target="tpu_custom_call" | custom-call | flops 115605504 | bytes 6291456 | tf_op jit(solution)/shard_map/project/pallas_call | solution.py:131
  51.3 0.5 collective-permute-start
  51.8 0.8 %collective-permute-done.b = f32[4,8,128]{2,1,0:T(8,128)S(1)} collective-permute-done((f32[4,8,128]{2,1,0:T(8,128)S(1)}, f32[4,8,128]{2,1,0:T(8,128)S(1)}, u32[]{:S(2)}, u32[]{:S(2)}) %collective-permute-start) | collective-permute-done | bytes 16416 | tf_op jit(solution)/shard_map/sum_u/ppermute | solution.py:341
  52.6 0.7 add_spread.1
  53.4 3.5 %all-to-all-start.3 = ((f32[16,4,8,128]{3,2,1,0:T(8,128)}), f32[16,4,8,128]{3,2,1,0:T(8,128)S(1)}, u32[]{:S(2)}, u32[]{:S(2)}) async-start(f32[16,4,8,128]{3,2,1,0:T(8,128)} %add_spread.1), calls=%async_computation.3 | async-start | bytes 524288 | tf_op jit(solution)/shard_map/sum_u/all_to_all | solution.py:360
  56.9 6.2 %ortho.1 = (f32[8,4096]{1,0:T(8,128)}, f32[8,8]{1,0:T(8,128)S(1)}, bf16[32,4096]{1,0:T(8,128)(2,1)S(1)}, bf16[624,1024]{1,0:T(8,128)(2,1)S(1)}, bf16[4096,1024]{1,0:T(8,128)(2,1)}) custom-call(f32[32,8,128]{2,1,0:T(8,128)S(1)} %all_to_all.27.p, f32[8,8,128]{2,1,0:T(8,128)S(1)} %get-tuple-element.20.u, bf16[592,1024]{1,0:T(8,128)(2,1)S(1)} %get-tuple-element.19.scaled, ...), custom_call_target="tpu_custom_call" | custom-call | flops 2466250752 | bytes 6291456 | tf_op jit(solution)/shard_map/ortho/pallas_call | solution.py:221
  63.2 1.4 %all-to-all-done.3.v = f32[16,4,8,128]{3,2,1,0:T(8,128)S(1)} async-done(((f32[16,4,8,128]{3,2,1,0:T(8,128)}), f32[16,4,8,128]{3,2,1,0:T(8,128)S(1)}, u32[]{:S(2)}, u32[]{:S(2)}) %all-to-all-start.3) | async-done | bytes 262176 | tf_op jit(solution)/shard_map/sum_u/all_to_all | solution.py:360
  64.6 0.7 spread.1
  65.3 3.5 %all-to-all-start.4 = ((f32[8,4,8,128]{3,2,1,0:T(8,128)}), f32[8,4,8,128]{3,2,1,0:T(8,128)S(1)}, u32[]{:S(2)}, u32[]{:S(2)}) async-start(f32[8,4,8,128]{3,2,1,0:T(8,128)} %spread.1), calls=%async_computation.4 | async-start | bytes 262144 | tf_op jit(solution)/shard_map/sum_u/all_to_all | solution.py:362
  68.8 7.3 %residual.1 = (bf16[4096,1024]{1,0:T(8,128)(2,1)}, f32[8,128]{1,0:T(8,128)S(1)}) custom-call(bf16[32,4096]{1,0:T(8,128)(2,1)S(1)} %get-tuple-element.26.lhs, bf16[624,1024]{1,0:T(8,128)(2,1)S(1)} %get-tuple-element.27.rhs, bf16[592,4096]{1,0:T(8,128)(2,1)} %get-tuple-element.21.act_h, ...), custom_call_target="tpu_custom_call", output_to_operand_aliasing={{0}: (3, {})} | custom-call | flops 4932501504 | bytes 14680064 | tf_op jit(solution)/shard_map/residual/pallas_call | solution.py:248
  76.1 0.4 all-to-all-done.4.v
  76.5 2.9 %collective-permute-start.1 = (f32[4,8,128]{2,1,0:T(8,128)S(1)}, f32[4,8,128]{2,1,0:T(8,128)S(1)}, u32[]{:S(2)}, u32[]{:S(2)}) collective-permute-start(f32[4,8,128]{2,1,0:T(8,128)S(1)} %total.1.mine), channel_id=1, source_target_pairs={{0,1},{1,0},{2,3},{3,2},{4,5},{5,4},{6,7},{7,6},{8,9},{9,8},{10,11... | collective-permute-start | bytes 49160 | tf_op jit(solution)/shard_map/sum_u/ppermute | solution.py:341
  79.5 0.8 %collective-permute-done.1.other = f32[4,8,128]{2,1,0:T(8,128)S(1)} collective-permute-done((f32[4,8,128]{2,1,0:T(8,128)S(1)}, f32[4,8,128]{2,1,0:T(8,128)S(1)}, u32[]{:S(2)}, u32[]{:S(2)}) %collective-permute-start.1) | collective-permute-done | bytes 16416 | tf_op jit(solution)/shard_map/sum_u/ppermute | solution.py:341
  80.3 0.8 finish.1
  (5 shorter events, 0.0 us)
Async XLA Ops:
  51.3 1.3 %collective-permute-start = (f32[4,8,128]{2,1,0:T(8,128)S(1)}, f32[4,8,128]{2,1,0:T(8,128)S(1)}, u32[]{:S(2)}, u32[]{:S(2)}) collective-permute-start(f32[4,8,128]{2,1,0:T(8,128)S(1)} %get-tuple-element.25), channel_id=1, source_target_pairs={{0,1},{1,0},{2,3},{3,2},{4,5},{5,4},{6,7},{7,6},{8,9},{9,8},{10,11... | collective-permute-start | bytes 49160 | tf_op jit(solution)/shard_map/sum_u/ppermute | solution.py:341
  53.4 11.2 %all-to-all-start.3 = ((f32[16,4,8,128]{3,2,1,0:T(8,128)}), f32[16,4,8,128]{3,2,1,0:T(8,128)S(1)}, u32[]{:S(2)}, u32[]{:S(2)}) async-start(f32[16,4,8,128]{3,2,1,0:T(8,128)} %add_spread.1), calls=%async_computation.3 | async-start | bytes 524288 | tf_op jit(solution)/shard_map/sum_u/all_to_all | solution.py:360
  65.3 11.2 %all-to-all-start.4 = ((f32[8,4,8,128]{3,2,1,0:T(8,128)}), f32[8,4,8,128]{3,2,1,0:T(8,128)S(1)}, u32[]{:S(2)}, u32[]{:S(2)}) async-start(f32[8,4,8,128]{3,2,1,0:T(8,128)} %spread.1), calls=%async_computation.4 | async-start | bytes 262144 | tf_op jit(solution)/shard_map/sum_u/all_to_all | solution.py:362
  76.5 3.8 %collective-permute-start.1 = (f32[4,8,128]{2,1,0:T(8,128)S(1)}, f32[4,8,128]{2,1,0:T(8,128)S(1)}, u32[]{:S(2)}, u32[]{:S(2)}) collective-permute-start(f32[4,8,128]{2,1,0:T(8,128)S(1)} %total.1.mine), channel_id=1, source_target_pairs={{0,1},{1,0},{2,3},{3,2},{4,5},{5,4},{6,7},{7,6},{8,9},{9,8},{10,11... | collective-permute-start | bytes 49160 | tf_op jit(solution)/shard_map/sum_u/ppermute | solution.py:341

commit v5 on v4

--- a/solution.py
+++ b/solution.py
@@ -14,8 +14,8 @@
 EVEN, AUG = 592, 624
 FRONT_LIMIT, RES_LIMIT = 52 << 20, 50 << 20
 BANDS = ((0, 64), (64, 256), (256, 512), (512, ROWS))
-SPANS_A = ((0, 768), (768, 1280))
-SPANS_B = ((1280, 1536), (1536, 2304), (2304, 3072), (3072, 3840), (3840, 4096))
+SPANS_A = ((0, 768), (768, 1536), (1536, 2048))
+SPANS_B = ((2048, 2304), (2304, 3072), (3072, 3840), (3840, 4096))
 PLANE = ("x", "y", "c")
 
 
@@ -356,10 +356,10 @@
     basis_out, inverse, lhs, rhs, early = ortho(p_total, u, scaled, act_h)
     residual, mark = residual_of(lhs, rhs, act_h, early)
     with jax.named_scope("sum_u"):
-        t = add_spread(keep, swap(send), 16)
-        t = lax.all_to_all(t, ("x", "y"), 0, 0, tiled=True)
-        t = spread(t, inverse, 8)
-        mine = total_after(lax.all_to_all(t, "z", 0, 0, tiled=True), mark)
+        t = add_spread(keep, swap(send), 8)
+        t = lax.all_to_all(t, "z", 0, 0, tiled=True)
+        t = spread(t, inverse, 16)
+        mine = total_after(lax.all_to_all(t, ("x", "y"), 0, 0, tiled=True), mark)
         other = swap(mine)
     q_out = finish(inverse, mine, other, 256)
     return (basis_out, q_out, residual)

time: 81.5 us -> 81.5 us (level)
    pallas_call x1, Pallas kernels: 6.24 us -> 7.7 us  [ortho(): pl.pallas_call(ortho_kernel, in_specs=[vmem, vmem, vmem, anywhere], out_s...]
    pallas_call x1, Pallas kernels: 7.29 us -> 5.91 us  [residual_of(): pl.pallas_call(residual_kernel, in_specs=[vmem, vmem, anywhere, anywhere]...]
where the time goes in v5:
time: 81.5 us; the launch traced here: 81.1 us
  blocking collectives  43.7 us (54%)
  Pallas kernels  22.8 us (28%)
  starting transfers between devices  10.4 us (13%)
  waiting for transfers between devices  3.51 us (4%)
    all_to_all x2, blocking collectives, gather_all_to_all(): return lax.all_to_all(copies, axes, 0, 0, tiled=True)  27.6 us
    all_to_all x1, blocking collectives, body(): part = total(lax.all_to_all(p_local, PLANE, 0, 0, tiled=True))  16.1 us
    pallas_call x1, Pallas kernels, ortho(): pl.pallas_call(ortho_kernel, in_specs=[vmem, vmem, vmem, anywhere], out_s...  7.7 us
    pallas_call x1, Pallas kernels, residual_of(): pl.pallas_call(residual_kernel, in_specs=[vmem, vmem, anywhere, anywhere]...  5.91 us
    pallas_call x1, Pallas kernels, front(): pl.pallas_call(functools.partial(front_kernel, slab, cols), in_specs=[pl....  5.01 us
    all_to_all x1, starting transfers between devices, body(): mine = total_after(lax.all_to_all(t, ('x', 'y'), 0, 0, tiled=True), mark)  3.71 us
    all_to_all x1, starting transfers between devices, body(): t = lax.all_to_all(t, 'z', 0, 0, tiled=True)  3.37 us
    ppermute x2, starting transfers between devices, swap(): return lax.ppermute(v, 'c', [(0, 1), (1, 0)])  3.32 us
  transfers between devices with their start and end apart: 4, of which 4 were waited for; matrix products, arithmetic and copies ran while one was open for 0% of the time, Pallas kernels for 17%

profile of v5, /device:TPU:1, one launch (start us, length us, event | category | flops | bytes accessed | tf_op | source)
XLA Modules:
  0.0 81.1 jit_solution(12400983892990696249)
XLA Ops:
  0.6 5.0 %front.1 = (bf16[592,4096]{1,0:T(8,128)(2,1)S(1)}, bf16[592,4096]{1,0:T(8,128)(2,1)}, bf16[592,1024]{1,0:T(8,128)(2,1)S(1)}, f32[32,8,128]{2,1,0:T(8,128)S(1)}) custom-call(bf16[588,4096]{1,0:T(8,128)(2,1)} %pre_h.1, bf16[588,1024]{1,0:T(8,128)(2,1)} %up_h.1, f32[1,1024]{1,0:T(1,128)} %bitcast.5, f32[8,1024]{1,0:T(8,128)} %q_h.1), custom_call_target="tpu_custom_call" | custom-call | flops 144506880 | bytes 10485760 | tf_op jit(solution)/shard_map/front/pallas_call | solution.py:87
  5.7 16.1 %all_to_all.25 = f32[32,8,128]{2,1,0:T(8,128)S(1)} all-to-all(f32[32,8,128]{2,1,0:T(8,128)S(1)} %get-tuple-element.17), channel_id=1, replica_groups=mesh['z'=8,'x'=4,'y'=4,'c'=2] {'x','y','c'}, dimensions={0} | all-to-all | bytes 262144 | tf_op jit(solution)/shard_map/sum_p/all_to_all | solution.py:352
  21.8 15.0 %all_to_all.26 = f32[8,8,128]{2,1,0:T(8,128)S(1)} all-to-all(f32[8,8,128]{2,1,0:T(8,128)S(1)} %reshape.255), channel_id=1, replica_groups=mesh['z'=8,'x'=4,'y'=4,'c'=2] {'z'}, dimensions={0} | all-to-all | bytes 65536 | tf_op jit(solution)/shard_map/sum_p/all_to_all | solution.py:346
  36.7 12.6 %all_to_all.27.p = f32[32,8,128]{2,1,0:T(8,128)S(1)} all-to-all(f32[32,8,128]{2,1,0:T(8,128)S(1)} %reshape.256), channel_id=1, replica_groups=mesh['z'=8,'x'=4,'y'=4,'c'=2] {'x','y','c'}, dimensions={0} | all-to-all | bytes 262144 | tf_op jit(solution)/shard_map/sum_p/all_to_all | solution.py:346
  49.4 1.9 %project.1 = (f32[8,8,128]{2,1,0:T(8,128)S(1)}, f32[4,8,128]{2,1,0:T(8,128)S(1)}, f32[4,8,128]{2,1,0:T(8,128)S(1)}) custom-call(bf16[592,4096]{1,0:T(8,128)(2,1)S(1)} %get-tuple-element.18.act, bf16[592,1024]{1,0:T(8,128)(2,1)S(1)} %get-tuple-element.19.scaled, f32[32,8,128]{2,1,0:T(8,128)S(1)} %all_to_all.27.p), custom_call_target="tpu_custom_call" | custom-call | flops 115605504 | bytes 6291456 | tf_op jit(solution)/shard_map/project/pallas_call | solution.py:131
  51.3 0.5 collective-permute-start
  51.8 0.8 %collective-permute-done.b = f32[4,8,128]{2,1,0:T(8,128)S(1)} collective-permute-done((f32[4,8,128]{2,1,0:T(8,128)S(1)}, f32[4,8,128]{2,1,0:T(8,128)S(1)}, u32[]{:S(2)}, u32[]{:S(2)}) %collective-permute-start) | collective-permute-done | bytes 16416 | tf_op jit(solution)/shard_map/sum_u/ppermute | solution.py:341
  52.6 0.7 add_spread.1
  53.3 3.4 %all-to-all-start.3 = ((f32[8,4,8,128]{3,2,1,0:T(8,128)}), f32[8,4,8,128]{3,2,1,0:T(8,128)S(1)}, u32[]{:S(2)}, u32[]{:S(2)}) async-start(f32[8,4,8,128]{3,2,1,0:T(8,128)} %add_spread.1), calls=%async_computation.3 | async-start | bytes 262144 | tf_op jit(solution)/shard_map/sum_u/all_to_all | solution.py:360
  56.7 7.7 %ortho.1 = (f32[8,4096]{1,0:T(8,128)}, f32[8,8]{1,0:T(8,128)S(1)}, bf16[32,4096]{1,0:T(8,128)(2,1)S(1)}, bf16[624,1024]{1,0:T(8,128)(2,1)S(1)}, bf16[4096,1024]{1,0:T(8,128)(2,1)}) custom-call(f32[32,8,128]{2,1,0:T(8,128)S(1)} %all_to_all.27.p, f32[8,8,128]{2,1,0:T(8,128)S(1)} %get-tuple-element.20.u, bf16[592,1024]{1,0:T(8,128)(2,1)S(1)} %get-tuple-element.19.scaled, ...), custom_call_target="tpu_custom_call" | custom-call | flops 2466250752 | bytes 6291456 | tf_op jit(solution)/shard_map/ortho/pallas_call | solution.py:221
  64.4 0.6 all-to-all-done.3.v
  65.0 0.7 spread.1
  65.8 3.7 %all-to-all-start.4 = ((f32[16,4,8,128]{3,2,1,0:T(8,128)}), f32[16,4,8,128]{3,2,1,0:T(8,128)S(1)}, u32[]{:S(2)}, u32[]{:S(2)}) async-start(f32[16,4,8,128]{3,2,1,0:T(8,128)} %spread.1), calls=%async_computation.4 | async-start | bytes 524288 | tf_op jit(solution)/shard_map/sum_u/all_to_all | solution.py:362
  69.5 5.9 %residual.1 = (bf16[4096,1024]{1,0:T(8,128)(2,1)}, f32[8,128]{1,0:T(8,128)S(1)}) custom-call(bf16[32,4096]{1,0:T(8,128)(2,1)S(1)} %get-tuple-element.26.lhs, bf16[624,1024]{1,0:T(8,128)(2,1)S(1)} %get-tuple-element.27.rhs, bf16[592,4096]{1,0:T(8,128)(2,1)} %get-tuple-element.21.act_h, ...), custom_call_target="tpu_custom_call", output_to_operand_aliasing={{0}: (3, {})} | custom-call | flops 4932501504 | bytes 14680064 | tf_op jit(solution)/shard_map/residual/pallas_call | solution.py:248
  75.4 1.2 %all-to-all-done.4.v = f32[16,4,8,128]{3,2,1,0:T(8,128)S(1)} async-done(((f32[16,4,8,128]{3,2,1,0:T(8,128)}), f32[16,4,8,128]{3,2,1,0:T(8,128)S(1)}, u32[]{:S(2)}, u32[]{:S(2)}) %all-to-all-start.4) | async-done | bytes 262176 | tf_op jit(solution)/shard_map/sum_u/all_to_all | solution.py:362
  76.6 2.8 %collective-permute-start.1 = (f32[4,8,128]{2,1,0:T(8,128)S(1)}, f32[4,8,128]{2,1,0:T(8,128)S(1)}, u32[]{:S(2)}, u32[]{:S(2)}) collective-permute-start(f32[4,8,128]{2,1,0:T(8,128)S(1)} %total.1.mine), channel_id=1, source_target_pairs={{0,1},{1,0},{2,3},{3,2},{4,5},{5,4},{6,7},{7,6},{8,9},{9,8},{10,11... | collective-permute-start | bytes 49160 | tf_op jit(solution)/shard_map/sum_u/ppermute | solution.py:341
  79.5 0.8 %collective-permute-done.1.other = f32[4,8,128]{2,1,0:T(8,128)S(1)} collective-permute-done((f32[4,8,128]{2,1,0:T(8,128)S(1)}, f32[4,8,128]{2,1,0:T(8,128)S(1)}, u32[]{:S(2)}, u32[]{:S(2)}) %collective-permute-start.1) | collective-permute-done | bytes 16416 | tf_op jit(solution)/shard_map/sum_u/ppermute | solution.py:341
  80.3 0.8 finish.1
  (5 shorter events, 0.1 us)
Async XLA Ops:
  51.3 1.3 %collective-permute-start = (f32[4,8,128]{2,1,0:T(8,128)S(1)}, f32[4,8,128]{2,1,0:T(8,128)S(1)}, u32[]{:S(2)}, u32[]{:S(2)}) collective-permute-start(f32[4,8,128]{2,1,0:T(8,128)S(1)} %get-tuple-element.25), channel_id=1, source_target_pairs={{0,1},{1,0},{2,3},{3,2},{4,5},{5,4},{6,7},{7,6},{8,9},{9,8},{10,11... | collective-permute-start | bytes 49160 | tf_op jit(solution)/shard_map/sum_u/ppermute | solution.py:341
  53.3 11.7 %all-to-all-start.3 = ((f32[8,4,8,128]{3,2,1,0:T(8,128)}), f32[8,4,8,128]{3,2,1,0:T(8,128)S(1)}, u32[]{:S(2)}, u32[]{:S(2)}) async-start(f32[8,4,8,128]{3,2,1,0:T(8,128)} %add_spread.1), calls=%async_computation.3 | async-start | bytes 262144 | tf_op jit(solution)/shard_map/sum_u/all_to_all | solution.py:360
  65.8 10.8 %all-to-all-start.4 = ((f32[16,4,8,128]{3,2,1,0:T(8,128)}), f32[16,4,8,128]{3,2,1,0:T(8,128)S(1)}, u32[]{:S(2)}, u32[]{:S(2)}) async-start(f32[16,4,8,128]{3,2,1,0:T(8,128)} %spread.1), calls=%async_computation.4 | async-start | bytes 524288 | tf_op jit(solution)/shard_map/sum_u/all_to_all | solution.py:362
  76.6 3.7 %collective-permute-start.1 = (f32[4,8,128]{2,1,0:T(8,128)S(1)}, f32[4,8,128]{2,1,0:T(8,128)S(1)}, u32[]{:S(2)}, u32[]{:S(2)}) collective-permute-start(f32[4,8,128]{2,1,0:T(8,128)S(1)} %total.1.mine), channel_id=1, source_target_pairs={{0,1},{1,0},{2,3},{3,2},{4,5},{5,4},{6,7},{7,6},{8,9},{9,8},{10,11... | collective-permute-start | bytes 49160 | tf_op jit(solution)/shard_map/sum_u/ppermute | solution.py:341

commit v6 on v4

--- a/solution.py
+++ b/solution.py
@@ -113,8 +113,8 @@
 def project_kernel(act, scaled, p, u_out, keep, send):
     flat = jnp.concatenate([p[j] for j in range(HID // LANES)], axis=1)
     c = lax.dot_general(
-        split3(flat), act[...], (((1,), (1,)), ((), ())), preferred_element_type=f32
-    )
+        act[...], split3(flat), (((1,), (1,)), ((), ())), preferred_element_type=f32
+    ).T
     u = fold3(jnp.dot(split3(fold3(c)), scaled[...], preferred_element_type=f32))
     core = lax.axis_index("c")
     half = WID // LANES // 2

time: 81.5 us -> 81.5 us (level)
  no operation moved by 1% of the time
where the time goes in v6:
time: 81.5 us; the launch traced here: 81.1 us
  blocking collectives  43.7 us (54%)
  Pallas kernels  22.7 us (28%)
  starting transfers between devices  10.5 us (13%)
  waiting for transfers between devices  3.5 us (4%)
    all_to_all x2, blocking collectives, gather_all_to_all(): return lax.all_to_all(copies, axes, 0, 0, tiled=True)  27.6 us
    all_to_all x1, blocking collectives, body(): part = total(lax.all_to_all(p_local, PLANE, 0, 0, tiled=True))  16.1 us
    pallas_call x1, Pallas kernels, residual_of(): pl.pallas_call(residual_kernel, in_specs=[vmem, vmem, anywhere, anywhere]...  7.29 us
    pallas_call x1, Pallas kernels, ortho(): pl.pallas_call(ortho_kernel, in_specs=[vmem, vmem, vmem, anywhere], out_s...  6.24 us
    pallas_call x1, Pallas kernels, front(): pl.pallas_call(functools.partial(front_kernel, slab, cols), in_specs=[pl....  5.01 us
    all_to_all x1, starting transfers between devices, body(): mine = total_after(lax.all_to_all(t, 'z', 0, 0, tiled=True), mark)  3.55 us
    all_to_all x1, starting transfers between devices, body(): t = lax.all_to_all(t, ('x', 'y'), 0, 0, tiled=True)  3.53 us
    ppermute x2, starting transfers between devices, swap(): return lax.ppermute(v, 'c', [(0, 1), (1, 0)])  3.4 us
  transfers between devices with their start and end apart: 4, of which 4 were waited for; matrix products, arithmetic and copies ran while one was open for 0% of the time, Pallas kernels for 17%

profile of v6, /device:TPU:1, one launch (start us, length us, event | category | flops | bytes accessed | tf_op | source)
XLA Modules:
  0.0 81.1 jit_solution(14372270632871323510)
XLA Ops:
  0.6 5.0 %front.1 = (bf16[592,4096]{1,0:T(8,128)(2,1)S(1)}, bf16[592,4096]{1,0:T(8,128)(2,1)}, bf16[592,1024]{1,0:T(8,128)(2,1)S(1)}, f32[32,8,128]{2,1,0:T(8,128)S(1)}) custom-call(bf16[588,4096]{1,0:T(8,128)(2,1)} %pre_h.1, bf16[588,1024]{1,0:T(8,128)(2,1)} %up_h.1, f32[1,1024]{1,0:T(1,128)} %bitcast.5, f32[8,1024]{1,0:T(8,128)} %q_h.1), custom_call_target="tpu_custom_call" | custom-call | flops 144506880 | bytes 10485760 | tf_op jit(solution)/shard_map/front/pallas_call | solution.py:87
  5.7 16.1 %all_to_all.25 = f32[32,8,128]{2,1,0:T(8,128)S(1)} all-to-all(f32[32,8,128]{2,1,0:T(8,128)S(1)} %get-tuple-element.17), channel_id=1, replica_groups=mesh['z'=8,'x'=4,'y'=4,'c'=2] {'x','y','c'}, dimensions={0} | all-to-all | bytes 262144 | tf_op jit(solution)/shard_map/sum_p/all_to_all | solution.py:352
  21.8 15.0 %all_to_all.26 = f32[8,8,128]{2,1,0:T(8,128)S(1)} all-to-all(f32[8,8,128]{2,1,0:T(8,128)S(1)} %reshape.255), channel_id=1, replica_groups=mesh['z'=8,'x'=4,'y'=4,'c'=2] {'z'}, dimensions={0} | all-to-all | bytes 65536 | tf_op jit(solution)/shard_map/sum_p/all_to_all | solution.py:346
  36.7 12.6 %all_to_all.27.p = f32[32,8,128]{2,1,0:T(8,128)S(1)} all-to-all(f32[32,8,128]{2,1,0:T(8,128)S(1)} %reshape.256), channel_id=1, replica_groups=mesh['z'=8,'x'=4,'y'=4,'c'=2] {'x','y','c'}, dimensions={0} | all-to-all | bytes 262144 | tf_op jit(solution)/shard_map/sum_p/all_to_all | solution.py:346
  49.4 1.9 %project.1 = (f32[8,8,128]{2,1,0:T(8,128)S(1)}, f32[4,8,128]{2,1,0:T(8,128)S(1)}, f32[4,8,128]{2,1,0:T(8,128)S(1)}) custom-call(bf16[592,4096]{1,0:T(8,128)(2,1)S(1)} %get-tuple-element.18.act, bf16[592,1024]{1,0:T(8,128)(2,1)S(1)} %get-tuple-element.19.scaled, f32[32,8,128]{2,1,0:T(8,128)S(1)} %all_to_all.27.p), custom_call_target="tpu_custom_call" | custom-call | flops 115605504 | bytes 6291456 | tf_op jit(solution)/shard_map/project/pallas_call | solution.py:131
  51.3 0.5 collective-permute-start
  51.8 0.8 %collective-permute-done.b = f32[4,8,128]{2,1,0:T(8,128)S(1)} collective-permute-done((f32[4,8,128]{2,1,0:T(8,128)S(1)}, f32[4,8,128]{2,1,0:T(8,128)S(1)}, u32[]{:S(2)}, u32[]{:S(2)}) %collective-permute-start) | collective-permute-done | bytes 16416 | tf_op jit(solution)/shard_map/sum_u/ppermute | solution.py:341
  52.6 0.7 add_spread.1
  53.4 3.5 %all-to-all-start.3 = ((f32[16,4,8,128]{3,2,1,0:T(8,128)}), f32[16,4,8,128]{3,2,1,0:T(8,128)S(1)}, u32[]{:S(2)}, u32[]{:S(2)}) async-start(f32[16,4,8,128]{3,2,1,0:T(8,128)} %add_spread.1), calls=%async_computation.3 | async-start | bytes 524288 | tf_op jit(solution)/shard_map/sum_u/all_to_all | solution.py:360
  56.9 6.2 %ortho.1 = (f32[8,4096]{1,0:T(8,128)}, f32[8,8]{1,0:T(8,128)S(1)}, bf16[32,4096]{1,0:T(8,128)(2,1)S(1)}, bf16[624,1024]{1,0:T(8,128)(2,1)S(1)}, bf16[4096,1024]{1,0:T(8,128)(2,1)}) custom-call(f32[32,8,128]{2,1,0:T(8,128)S(1)} %all_to_all.27.p, f32[8,8,128]{2,1,0:T(8,128)S(1)} %get-tuple-element.20.u, bf16[592,1024]{1,0:T(8,128)(2,1)S(1)} %get-tuple-element.19.scaled, ...), custom_call_target="tpu_custom_call" | custom-call | flops 2466250752 | bytes 6291456 | tf_op jit(solution)/shard_map/ortho/pallas_call | solution.py:221
  63.2 1.5 %all-to-all-done.3.v = f32[16,4,8,128]{3,2,1,0:T(8,128)S(1)} async-done(((f32[16,4,8,128]{3,2,1,0:T(8,128)}), f32[16,4,8,128]{3,2,1,0:T(8,128)S(1)}, u32[]{:S(2)}, u32[]{:S(2)}) %all-to-all-start.3) | async-done | bytes 262176 | tf_op jit(solution)/shard_map/sum_u/all_to_all | solution.py:360
  64.6 0.7 spread.1
  65.3 3.5 %all-to-all-start.4 = ((f32[8,4,8,128]{3,2,1,0:T(8,128)}), f32[8,4,8,128]{3,2,1,0:T(8,128)S(1)}, u32[]{:S(2)}, u32[]{:S(2)}) async-start(f32[8,4,8,128]{3,2,1,0:T(8,128)} %spread.1), calls=%async_computation.4 | async-start | bytes 262144 | tf_op jit(solution)/shard_map/sum_u/all_to_all | solution.py:362
  68.8 7.3 %residual.1 = (bf16[4096,1024]{1,0:T(8,128)(2,1)}, f32[8,128]{1,0:T(8,128)S(1)}) custom-call(bf16[32,4096]{1,0:T(8,128)(2,1)S(1)} %get-tuple-element.26.lhs, bf16[624,1024]{1,0:T(8,128)(2,1)S(1)} %get-tuple-element.27.rhs, bf16[592,4096]{1,0:T(8,128)(2,1)} %get-tuple-element.21.act_h, ...), custom_call_target="tpu_custom_call", output_to_operand_aliasing={{0}: (3, {})} | custom-call | flops 4932501504 | bytes 14680064 | tf_op jit(solution)/shard_map/residual/pallas_call | solution.py:248
  76.1 0.4 all-to-all-done.4.v
  76.5 2.9 %collective-permute-start.1 = (f32[4,8,128]{2,1,0:T(8,128)S(1)}, f32[4,8,128]{2,1,0:T(8,128)S(1)}, u32[]{:S(2)}, u32[]{:S(2)}) collective-permute-start(f32[4,8,128]{2,1,0:T(8,128)S(1)} %total.1.mine), channel_id=1, source_target_pairs={{0,1},{1,0},{2,3},{3,2},{4,5},{5,4},{6,7},{7,6},{8,9},{9,8},{10,11... | collective-permute-start | bytes 49160 | tf_op jit(solution)/shard_map/sum_u/ppermute | solution.py:341
  79.5 0.8 %collective-permute-done.1.other = f32[4,8,128]{2,1,0:T(8,128)S(1)} collective-permute-done((f32[4,8,128]{2,1,0:T(8,128)S(1)}, f32[4,8,128]{2,1,0:T(8,128)S(1)}, u32[]{:S(2)}, u32[]{:S(2)}) %collective-permute-start.1) | collective-permute-done | bytes 16416 | tf_op jit(solution)/shard_map/sum_u/ppermute | solution.py:341
  80.3 0.8 finish.1
  (5 shorter events, 0.0 us)
Async XLA Ops:
  51.3 1.3 %collective-permute-start = (f32[4,8,128]{2,1,0:T(8,128)S(1)}, f32[4,8,128]{2,1,0:T(8,128)S(1)}, u32[]{:S(2)}, u32[]{:S(2)}) collective-permute-start(f32[4,8,128]{2,1,0:T(8,128)S(1)} %get-tuple-element.25), channel_id=1, source_target_pairs={{0,1},{1,0},{2,3},{3,2},{4,5},{5,4},{6,7},{7,6},{8,9},{9,8},{10,11... | collective-permute-start | bytes 49160 | tf_op jit(solution)/shard_map/sum_u/ppermute | solution.py:341
  53.4 11.2 %all-to-all-start.3 = ((f32[16,4,8,128]{3,2,1,0:T(8,128)}), f32[16,4,8,128]{3,2,1,0:T(8,128)S(1)}, u32[]{:S(2)}, u32[]{:S(2)}) async-start(f32[16,4,8,128]{3,2,1,0:T(8,128)} %add_spread.1), calls=%async_computation.3 | async-start | bytes 524288 | tf_op jit(solution)/shard_map/sum_u/all_to_all | solution.py:360
  65.3 11.2 %all-to-all-start.4 = ((f32[8,4,8,128]{3,2,1,0:T(8,128)}), f32[8,4,8,128]{3,2,1,0:T(8,128)S(1)}, u32[]{:S(2)}, u32[]{:S(2)}) async-start(f32[8,4,8,128]{3,2,1,0:T(8,128)} %spread.1), calls=%async_computation.4 | async-start | bytes 262144 | tf_op jit(solution)/shard_map/sum_u/all_to_all | solution.py:362
  76.5 3.8 %collective-permute-start.1 = (f32[4,8,128]{2,1,0:T(8,128)S(1)}, f32[4,8,128]{2,1,0:T(8,128)S(1)}, u32[]{:S(2)}, u32[]{:S(2)}) collective-permute-start(f32[4,8,128]{2,1,0:T(8,128)S(1)} %total.1.mine), channel_id=1, source_target_pairs={{0,1},{1,0},{2,3},{3,2},{4,5},{5,4},{6,7},{7,6},{8,9},{9,8},{10,11... | collective-permute-start | bytes 49160 | tf_op jit(solution)/shard_map/sum_u/ppermute | solution.py:341
